TPU v7x, 512 devices: a whole 4x8x8 slice. The times are simulated.
512 devices in a mesh: rep: 32 (over x, z_lo, core), fsdp: 16 (over y, z_hi).
Axes of the slice: x: 4, y: 8, z: 8 (z_hi: 2, z_lo: 4; z = z_hi * 4 + z_lo), core: 2. Of those that a mesh axis runs over, the one named last changes fastest.
Arguments:
- activations: bfloat16 [32, 4096, 4608], P('rep', 'fsdp'), may hold values from -6 to 6
- weights: float32 [32, 4608, 384], P('rep', 'fsdp'), may hold values from -8 to 8
- momentum: float32 [32, 4608, 384], P('rep', 'fsdp'), may hold values from -3 to 3
- cotangent: bfloat16 [32, 4096, 128], P('rep', 'fsdp'), may hold values from -6 to 6
- step: int32 [1], replicated, may hold values from 0 to 63
Outputs:
- new_weights: float32 [32, 4608, 384], P('rep', 'fsdp')
- new_momentum: float32 [32, 4608, 384], P('rep', 'fsdp')
All inputs are finite; a program needn't handle non-finite values.
Results may differ from a plain program's by a relative error of at most 0.023.
Values may be sent and summed in bfloat16 or wider, within the bound.
A program may use at most 64 MiB of HBM per device.

v0:
```python
import jax
import jax.numpy as jnp
from jax import lax
from jax.sharding import PartitionSpec as P

HEADS = 32
PERIOD = 4


SOFT_CAP = 50.0
ROPE_BASE = 10000.0
MOMENTUM_DECAY = 0.9
LEARNING_RATE = 0.5


def for_sending(shard):
    return jax.tree.map(lambda a: a.astype(jnp.bfloat16) if a.dtype == jnp.float32 else a, shard)


def passed_along(value, axis, steps):
    count = lax.axis_size(axis)
    pairs = [(source, (source + steps) % count) for source in range(count)]
    return lax.ppermute(value, axis, pairs)


def rotate(matrix, positions, direction):
    half = matrix.shape[1] // 2
    freqs = ROPE_BASE ** (-(jnp.arange(half, dtype=jnp.float32) * 2.0 / matrix.shape[1]))
    angles = positions[:, None] * freqs[None, :]
    cosine = jnp.cos(angles)
    sine = jnp.sin(angles)
    first = matrix[:, :half]
    second = matrix[:, half:]
    return jnp.concatenate(
        [first * cosine - direction * second * sine, second * cosine + direction * first * sine],
        axis=1,
    )


def inner_last(left, right):
    return lax.dot_general(
        left, right, (((1,), (1,)), ((), ())), preferred_element_type=jnp.float32
    )


def inner_first(left, right):
    return lax.dot_general(
        left, right, (((0,), (0,)), ((), ())), preferred_element_type=jnp.float32
    )


def score_block(left, right, left_pos, right_pos, qscale):
    tangent = jnp.tanh(inner_last(left, right) * qscale / SOFT_CAP)
    causal = left_pos[:, None] >= right_pos[None, :]
    expo = jnp.where(causal, jnp.exp(SOFT_CAP * tangent), jnp.float32(0.0))
    return (tangent, expo)


def shifter(by_count):

    def shifted(stepped):
        return jax.tree.map(
            lambda part, own: part.astype(own.dtype),
            passed_along(for_sending(stepped), "rep", by_count),
            stepped,
        )

    return shifted


def on_device(activations, weights, momentum, cotangent, step):
    acts = activations[0]
    params = weights[0]
    moment = momentum[0]
    grad_out = cotangent[0]
    tok_here = acts.shape[0]
    width = acts.shape[1]
    head_size = grad_out.shape[1]
    qscale = float(width // HEADS) ** (-0.5)
    own_index = lax.axis_index("fsdp") * tok_here + jnp.arange(tok_here, dtype=jnp.int32)
    own_pos = own_index.astype(jnp.float32)
    columns = acts
    proj = jnp.dot(
        columns,
        lax.all_gather(params.astype(jnp.bfloat16), "fsdp", axis=0, tiled=True),
        preferred_element_type=jnp.float32,
    )
    proj = proj * float(width) ** (-0.5)
    query_rot = rotate(proj[:, :head_size], own_pos, 1.0).astype(jnp.bfloat16)
    key_rot = rotate(proj[:, head_size : 2 * head_size], own_pos, 1.0).astype(jnp.bfloat16)
    values = proj[:, 2 * head_size :].astype(jnp.bfloat16)
    key_piece = lax.all_gather(key_rot, "fsdp", axis=0, tiled=True)
    value_piece = lax.all_gather(values, "fsdp", axis=0, tiled=True)
    key_index = jnp.arange(key_piece.shape[0], dtype=jnp.int32)
    tangent, expo = score_block(query_rot, key_piece, own_index, key_index, qscale)
    weighted = jnp.dot(expo.astype(jnp.bfloat16), value_piece, preferred_element_type=jnp.float32)
    weighted, row_total = (weighted, jnp.sum(expo, axis=1))
    output = (weighted / row_total[:, None]).astype(jnp.bfloat16)
    delta = jnp.sum(grad_out.astype(jnp.float32) * output.astype(jnp.float32), axis=1)
    key_piece = lax.all_gather(key_rot, "fsdp", axis=0, tiled=True)
    value_piece = lax.all_gather(values, "fsdp", axis=0, tiled=True)
    key_index = jnp.arange(key_piece.shape[0], dtype=jnp.int32)
    tangent, expo = score_block(query_rot, key_piece, own_index, key_index, qscale)
    prob = expo / row_total[:, None]
    dprob = inner_last(grad_out, value_piece)
    dscore = (prob * (dprob - delta[:, None]) * (1.0 - tangent * tangent) * qscale).astype(
        jnp.bfloat16
    )
    dquery_rot = jnp.dot(dscore, key_piece, preferred_element_type=jnp.float32)
    query_piece = lax.all_gather(
        query_rot.astype(jnp.float32).astype(jnp.bfloat16), "fsdp", axis=0, tiled=True
    )
    grad_piece = lax.all_gather(
        grad_out.astype(jnp.float32).astype(jnp.bfloat16), "fsdp", axis=0, tiled=True
    )
    total_piece = lax.all_gather(row_total.astype(jnp.bfloat16), "fsdp", axis=0, tiled=True).astype(
        jnp.float32
    )
    delta_piece = lax.all_gather(delta.astype(jnp.bfloat16), "fsdp", axis=0, tiled=True).astype(
        jnp.float32
    )
    query_index = jnp.arange(query_piece.shape[0], dtype=jnp.int32)
    tangent, expo = score_block(query_piece, key_rot, query_index, own_index, qscale)
    prob = expo / total_piece[:, None]
    dvalue_sum = inner_first(prob.astype(jnp.bfloat16), grad_piece)
    dprob = inner_last(grad_piece, values)
    dscore = (prob * (dprob - delta_piece[:, None]) * (1.0 - tangent * tangent) * qscale).astype(
        jnp.bfloat16
    )
    dkey_rot, dvalue_sum = (inner_first(dscore, query_piece), dvalue_sum)
    dquery = rotate(dquery_rot, own_pos, -1.0).astype(jnp.bfloat16)
    dkey = rotate(dkey_rot, own_pos, -1.0).astype(jnp.bfloat16)
    dproj = jnp.concatenate([dquery, dkey, dvalue_sum.astype(jnp.bfloat16)], axis=1)
    columns = acts
    grad = lax.psum_scatter(
        (inner_first(columns, dproj) * float(width) ** (-0.5)).astype(jnp.bfloat16),
        "fsdp",
        scatter_dimension=0,
        tiled=True,
    ).astype(jnp.float32)
    new_moment = MOMENTUM_DECAY * moment + grad
    stepped = params - LEARNING_RATE * new_moment
    replicas = lax.axis_size("rep")
    branches = [shifter(2**level % replicas) for level in range(PERIOD)]
    partner = lax.switch(step[0] % PERIOD, branches, stepped)
    new_weights = (stepped + partner) * 0.5
    return (new_weights[None], new_moment[None])


def solution(mesh):
    in_specs = (
        P("rep", "fsdp", None),
        P("rep", "fsdp", None),
        P("rep", "fsdp", None),
        P("rep", "fsdp", None),
        P(),
    )
    out_specs = (P("rep", "fsdp", None), P("rep", "fsdp", None))
    return jax.shard_map(
        on_device, mesh=mesh, in_specs=in_specs, out_specs=out_specs, check_vma=False
    )
```

profile of v0, /device:TPU:16, one launch (start us, length us, event | category | flops | bytes accessed | tf_op | source)
XLA Modules:
  0.0 775.7 jit_solution(6191407013796525392)
XLA Ops:
  7.2 0.0 copy-start
  7.2 0.0 all-gather.9.cloned.1.call-start
  7.2 1.9 bitcast_convert_fusion
  9.1 0.0 all-gather.9.cloned.1.call-update
  9.1 0.0 all-gather.11.cloned.1.call-start
  9.2 131.8 %all-gather.9.cloned.1.call-done = bf16[4608,384]{1,0:T(8,128)(2,1)} async-done(((bf16[288,384]{1,0:T(8,128)(2,1)}), bf16[4608,384]{1,0:T(8,128)(2,1)}) %all-gather.9.cloned.1.call-update) | async-done | bytes 3538960 | tf_op jit(solution)/shard_map/all_gather | solution.py:85
  141.0 3.5 fusion.26
  144.5 0.0 copy-start.3
  144.5 0.3 fusion.71
  144.9 0.6 pad_maximum_fusion.1
  145.5 0.0 all-gather.11.cloned.1.call-update
  145.5 0.0 all-gather.13.cloned.1.call-start
  145.6 0.6 slice.85
  146.2 0.1 all-gather.13.cloned.1.call-update
  146.3 0.0 all-gather.15.cloned.1.call-start
  146.3 0.6 pad_maximum_fusion
  147.0 0.0 all-gather.15.cloned.1.call-update
  147.0 0.0 all-gather.17.cloned.1.call-start
  147.0 0.5 all-gather.17.cloned.1.call-update
  147.6 0.0 reduce-scatter.4.cloned.1.call-start
  147.6 0.1 copy.28
  147.8 84.4 %all-gather.11.cloned.1.call-done = bf16[4096,128]{0,1:T(8,128)(2,1)} async-done(((bf16[256,128]{0,1:T(8,128)(2,1)}), bf16[4096,128]{0,1:T(8,128)(2,1)}) %all-gather.11.cloned.1.call-update) | async-done | bytes 1048592 | tf_op jit(solution)/shard_map/all_gather | solution.py:100
  232.1 4.8 fusion.15
  236.9 84.7 %all-gather.13.cloned.1.call-done = bf16[4096,128]{0,1:T(8,128)(2,1)} async-done(((bf16[256,128]{0,1:T(8,128)(2,1)}), bf16[4096,128]{0,1:T(8,128)(2,1)}) %all-gather.13.cloned.1.call-update) | async-done | bytes 1048592 | tf_op jit(solution)/shard_map/all_gather | solution.py:101
  321.6 3.6 fusion.47
  325.2 41.9 %all-gather.2 = bf16[16,1,256]{2,1,0:T(2,128)(2,1)S(1)} all-gather(bf16[1,1,256]{2,1,0:T(2,128)(2,1)S(1)} %reshape.30), channel_id=1, replica_groups=mesh['rep'=32,'fsdp'=16] {'fsdp'}, dimensions={0}, use_global_device_ids=true | all-gather | bytes 8704 | tf_op jit(solution)/shard_map/all_gather | solution.py:119
  367.1 0.6 convert_element_type.116
  367.7 51.7 %all-gather.1 = bf16[16,1,256]{2,1,0:T(2,128)(2,1)S(1)} all-gather(bf16[1,1,256]{2,1,0:T(2,128)(2,1)S(1)} %reshape.28), channel_id=1, replica_groups=mesh['rep'=32,'fsdp'=16] {'fsdp'}, dimensions={0}, use_global_device_ids=true | all-gather | bytes 8704 | tf_op jit(solution)/shard_map/all_gather | solution.py:116
  419.4 0.6 convert_element_type.115
  420.0 5.0 fusion.25
  425.0 0.3 fusion.91
  425.4 0.3 fusion.90
  425.7 0.7 copy-done.4
  426.4 4.0 fusion.10
  430.4 70.7 %all-gather.17.cloned.1.call-done = bf16[1,4096,128]{2,1,0:T(8,128)(2,1)} async-done(((bf16[1,256,128]{2,1,0:T(8,128)(2,1)}), bf16[1,4096,128]{2,1,0:T(8,128)(2,1)}) %all-gather.17.cloned.1.call-update) | async-done | bytes 1048592 | tf_op jit(solution)/shard_map/all_gather | solution.py:113
  501.1 4.7 fusion.24
  505.9 0.9 fusion.89
  506.8 0.9 fusion.88
  507.7 4.7 fusion.32
  512.4 3.8 fusion.1
  516.2 5.8 copy.35
  522.0 0.0 reduce-scatter.4.cloned.1.call-update
  522.7 232.1 %reduce-scatter.4.cloned.1.call-done = bf16[288,384]{1,0:T(8,128)(2,1)} async-done(((bf16[4608,384]{1,0:T(8,128)(2,1)}), bf16[288,384]{1,0:T(8,128)(2,1)}) %reduce-scatter.4.cloned.1.call-update) | async-done | bytes 221200 | tf_op jit(solution)/shard_map/reduce_scatter | solution.py:135
  754.8 2.0 fusion.53
  756.7 11.3 %conditional.4 = (f32[288,384]{1,0:T(8,128)S(1)}) conditional(s32[]{:T(128)} %clamp.3, f32[288,384]{1,0:T(8,128)S(1)} %get-tuple-element.20, f32[288,384]{1,0:T(8,128)S(1)} %get-tuple-element.20, f32[288,384]{1,0:T(8,128)S(1)} %get-tuple-element.20, f32[288,384]{1,0:T(8,128)S(1)} %get-tuple-element.20), branch_computations={%region_3.4_spmd, %region_4.5_spmd, %region_5.6_spmd, %region_6.7_... | conditional | flops 221184 | bytes 2211888
  756.8 2.3 collective-permute-start.2
  759.1 9.0 %collective-permute-done.2 = bf16[288,384]{1,0:T(8,128)(2,1)S(1)} collective-permute-done((bf16[288,384]{1,0:T(8,128)(2,1)S(1)}, bf16[288,384]{1,0:T(8,128)(2,1)S(1)}, u32[]{:S(2)}, u32[]{:S(2)}) %collective-permute-start.2) | collective-permute-done | bytes 221216 | tf_op jit(solution)/shard_map/cond/branch_2_fun/ppermute | solution.py:23
  768.1 0.8 multiply_bitcast_fusion
  (19 shorter events, 0.1 us)
Async XLA Ops:
  7.2 133.9 %copy-start = (bf16[1,256,4608]{2,1,0:T(8,128)(2,1)S(1)}, bf16[1,256,4608]{2,1,0:T(8,128)(2,1)}, u32[]{:S(2)}) copy-start(bf16[1,256,4608]{2,1,0:T(8,128)(2,1)} %param.9) | copy-start | bytes 7077892
  7.2 140.5 %copy-start.5 = (bf16[1,256,128]{2,1,0:T(8,128)(2,1)S(1)}, bf16[1,256,128]{2,1,0:T(8,128)(2,1)}, u32[]{:S(2)}) copy-start(bf16[1,256,128]{2,1,0:T(8,128)(2,1)} %param.12) | copy-start | bytes 196612
  7.2 133.8 %all-gather.9.cloned.1.call-start = ((), (), s32[]{:S(2)}) async-start(), calls=%async_computation.1 | async-start | bytes 3760128 | tf_op jit(solution)/shard_map/all_gather | solution.py:85
  9.1 223.0 %all-gather.11.cloned.1.call-start = ((), (), s32[]{:S(2)}) async-start(), calls=%async_computation.2 | async-start | bytes 1114112 | tf_op jit(solution)/shard_map/all_gather | solution.py:100
  144.5 92.4 %copy-start.3 = (f32[256,384]{0,1:T(8,128)}, f32[256,384]{0,1:T(8,128)S(1)}, u32[]{:S(2)}) copy-start(f32[256,384]{0,1:T(8,128)S(1)} %fusion.26) | copy-start | bytes 1179652
  145.5 176.1 %all-gather.13.cloned.1.call-start = ((), (), s32[]{:S(2)}) async-start(), calls=%async_computation.3 | async-start | bytes 1114112 | tf_op jit(solution)/shard_map/all_gather | solution.py:101
  146.3 280.1 %all-gather.15.cloned.1.call-start = ((), (), s32[]{:S(2)}) async-start(), calls=%async_computation.4 | async-start | bytes 1114112 | tf_op jit(solution)/shard_map/all_gather | solution.py:110
  147.0 354.1 %all-gather.17.cloned.1.call-start = ((), (), s32[]{:S(2)}) async-start(), calls=%async_computation.5 | async-start | bytes 1114112 | tf_op jit(solution)/shard_map/all_gather | solution.py:113
  147.6 607.2 %reduce-scatter.4.cloned.1.call-start = ((), (), s32[]{:S(2)}) async-start(), calls=%async_computation.6 | async-start | bytes 3760128 | tf_op jit(solution)/shard_map/reduce_scatter | solution.py:135
  425.7 0.7 copy-start.4
  426.4 74.7 %copy-start.1 = (bf16[4096,128]{0,1:T(8,128)(2,1)S(1)}, bf16[4096,128]{0,1:T(8,128)(2,1)}, u32[]{:S(2)}) copy-start(bf16[4096,128]{0,1:T(8,128)(2,1)} %all-gather.15.cloned.1.call-done) | copy-start | bytes 3145732
  516.2 238.5 %copy-start.2 = (f32[1,288,384]{2,1,0:T(8,128)S(1)}, f32[1,288,384]{2,1,0:T(8,128)}, u32[]{:S(2)}) copy-start(f32[1,288,384]{2,1,0:T(8,128)} %param.10) | copy-start | bytes 1327108
  756.8 11.3 %collective-permute-start.2 = (bf16[288,384]{1,0:T(8,128)(2,1)S(1)}, bf16[288,384]{1,0:T(8,128)(2,1)S(1)}, u32[]{:S(2)}, u32[]{:S(2)}) collective-permute-start(bf16[288,384]{1,0:T(8,128)(2,1)S(1)} %convert_element_type.77), channel_id=1, source_target_pairs={{0,64},{16,80},{32,96},{48,112},{64,128},{80,144},{96,160},{112,17... | collective-permute-start | bytes 663560 | tf_op jit(solution)/shard_map/cond/branch_2_fun/ppermute | solution.py:23
Sparse Core Ops, SparseCore 0:
  11.8 129.1 all-gather.8
  145.7 86.4 all-gather.10
  235.2 86.3 all-gather.12
  324.6 86.3 all-gather.14
  414.0 87.0 all-gather.16
  522.1 232.5 reduce-scatter.3
where the time goes:
time: 776 us
  waiting for transfers between devices  613 us (79%)
  blocking collectives  93.6 us (12%)
  matrix products  34.1 us (4%)
  between operations  14.9 us (2%)
  other arithmetic  10.1 us (1%)
    reduce_scatter x1, waiting for transfers between devices, on_device(): lax.psum_scatter((inner_first(columns, dproj) * float(width) ** (-0.5)).a...  232 us
    all_gather x1, waiting for transfers between devices, on_device(): lax.all_gather(params.astype(jnp.bfloat16), 'fsdp', axis=0, tiled=True)  132 us
    all_gather x1, waiting for transfers between devices, on_device(): value_piece = lax.all_gather(values, 'fsdp', axis=0, tiled=True)  84.7 us
    all_gather x1, waiting for transfers between devices, on_device(): key_piece = lax.all_gather(key_rot, 'fsdp', axis=0, tiled=True)  84.4 us
    all_gather x1, waiting for transfers between devices, on_device(): lax.all_gather(grad_out.astype(jnp.float32).astype(jnp.bfloat16), 'fsdp',...  70.7 us
    all_gather x1, blocking collectives, on_device(): lax.all_gather(row_total.astype(jnp.bfloat16), 'fsdp', axis=0, tiled=True)  51.7 us
    all_gather x1, blocking collectives, on_device(): lax.all_gather(delta.astype(jnp.bfloat16), 'fsdp', axis=0, tiled=True)  41.9 us
  transfers between devices with their start and end apart: 7, of which 6 were waited for; matrix products, arithmetic and copies ran while one was open for 3% of the time, Pallas kernels for 0%

commit v1 on v0

v1 whole, which is shorter than its diff:
```python
import functools

import jax
import jax.numpy as jnp
import numpy as np
from jax import lax
from jax.experimental import pallas as pl
from jax.experimental.pallas import tpu as pltpu
from jax.sharding import PartitionSpec as P

HEADS = 32
PERIOD = 4
SOFT_CAP = 50.0
ROPE_BASE = 10000.0
MOMENTUM_DECAY = 0.9
LEARNING_RATE = 0.5
RING = 8
BF16 = jnp.bfloat16
F32 = jnp.float32
MESH = pl.DeviceIdType.MESH


def dot_nn(left, right):
    return lax.dot_general(left, right, (((1,), (0,)), ((), ())), preferred_element_type=F32)


def dot_nt(left, right):
    return lax.dot_general(left, right, (((1,), (1,)), ((), ())), preferred_element_type=F32)


def dot_tn(left, right):
    return lax.dot_general(left, right, (((0,), (0,)), ((), ())), preferred_element_type=F32)


def hops_of(direction, half):
    return RING // 2 if half == direction else RING // 2 - 1


class Gather:
    def __init__(self, buffer, rows, place, send_sem, recv_sem, base, y, device):
        self.buffer, self.rows, self.place = buffer, rows, place
        self.send_sem, self.recv_sem, self.base = send_sem, recv_sem, base
        self.y, self.device = y, device

    def copy(self, hop, direction, half, arriving):
        sign = 1 if direction == 0 else RING - 1
        back = hop if arriving else hop - 1
        source = lax.rem(self.y + (RING - sign) * back, RING)
        part = self.rows // 2
        start = pl.multiple_of(self.place(source) + half * part, 16)
        view = self.buffer.at[pl.ds(start, part), :]
        slot = self.base + ((hop - 1) * 2 + direction) * 2 + half
        return pltpu.make_async_remote_copy(
            src_ref=view,
            dst_ref=view,
            send_sem=self.send_sem.at[slot],
            recv_sem=self.recv_sem.at[slot],
            device_id=self.device(lax.rem(self.y + sign, RING)),
            device_id_type=MESH,
        )

    def units(self, hop):
        order = [(0, 0), (1, 1), (0, 1), (1, 0)]
        return [(d, h) for d, h in order if 1 <= hop <= hops_of(d, h)]

    def start(self):
        for direction, half in self.units(1):
            self.copy(1, direction, half, False).start()

    def relay(self, hop):
        for direction, half in self.units(hop):
            self.copy(hop, direction, half, True).wait_recv()
            if hop < hops_of(direction, half):
                self.copy(hop + 1, direction, half, False).start()

    def drain(self):
        for hop in range(1, RING // 2 + 1):
            for direction, half in self.units(hop):
                self.copy(hop, direction, half, False).wait_send()


class Scatter:
    def __init__(self, own, outgoing, incoming, send_sem, recv_sem, base, y, device):
        self.own, self.outgoing, self.incoming = own, outgoing, incoming
        self.send_sem, self.recv_sem, self.base = send_sem, recv_sem, base
        self.y, self.device = y, device

    def copy(self, step, direction, half):
        sign = 1 if direction == 0 else RING - 1
        index = (step * 2 + direction) * 2 + half
        return pltpu.make_async_remote_copy(
            src_ref=self.outgoing.at[index],
            dst_ref=self.incoming.at[index],
            send_sem=self.send_sem.at[self.base + index],
            recv_sem=self.recv_sem.at[self.base + index],
            device_id=self.device(lax.rem(self.y + sign, RING)),
            device_id_type=MESH,
        )

    def units(self, step):
        order = [(0, 0), (1, 1), (0, 1), (1, 0)]
        return [(d, h) for d, h in order if RING // 2 - step <= hops_of(d, h)]

    def step(self, step):
        for direction, half in self.units(step):
            sign = 1 if direction == 0 else RING - 1
            target = lax.rem(self.y + sign * (RING // 2 - step), RING)
            total = self.own(target, half)
            if step > 0 and (direction, half) in self.units(step - 1):
                self.copy(step - 1, direction, half).wait_recv()
                total += self.incoming[((step - 1) * 2 + direction) * 2 + half].astype(F32)
            self.outgoing[(step * 2 + direction) * 2 + half] = total.astype(BF16)
            self.copy(step, direction, half).start()

    def result(self, half):
        last = RING // 2 - 1
        total = self.own(self.y, half)
        for direction in range(2):
            self.copy(last, direction, half).wait_recv()
            total += self.incoming[(last * 2 + direction) * 2 + half].astype(F32)
        return total

    def drain(self):
        for step in range(RING // 2):
            for direction, half in self.units(step):
                self.copy(step, direction, half).wait_send()


W_OWN, W_PAIR, DOUT, QUERY, DQUERY, G_PAIR, G_OWN = range(0, 7 * 16, 16)
Z_W, Z_KV, Z_DKV, Z_G = 112, 114, 116, 118
STATS = 120
SEMS = 128


def kernel(
    acts_hbm,
    weights_ref,
    momentum_hbm,
    dout_ref,
    near_ref,
    far_ref,
    new_momentum_ref,
    stepped_ref,
    acts,
    acts_t,
    momentum,
    wall,
    dout_all,
    query_all,
    kv_all,
    expo_buf,
    slope_buf,
    dprob_buf,
    stats_own,
    stats_in,
    dq_buf,
    dq_out,
    dq_in,
    dkv_acc,
    dkv_out,
    dkv_in,
    dproj,
    g_out_pair,
    g_in_pair,
    g_out_own,
    g_in_own,
    z_out,
    z_in,
    send_sem,
    recv_sem,
    local_sem,
):
    rows = weights_ref.shape[0]
    tokens, head = dout_ref.shape
    width = acts.shape[1]
    qscale = float(width // HEADS) ** (-0.5)
    pscale = float(width) ** (-0.5)

    place = lax.axis_index("fsdp")
    y = lax.div(place, 2)
    zh = lax.rem(place, 2)

    def column(row):
        return {"fsdp": row * 2 + zh}

    pair = {"fsdp": y * 2 + (1 - zh)}

    acts_copy = pltpu.make_async_copy(acts_hbm, acts, local_sem.at[0])
    acts_copy.start()
    momentum_copy = pltpu.make_async_copy(momentum_hbm, momentum, local_sem.at[1])
    momentum_copy.start()

    barrier = pltpu.get_barrier_semaphore()
    for ahead in range(1, RING):
        pl.semaphore_signal(
            barrier, inc=1, device_id=column(lax.rem(y + ahead, RING)), device_id_type=MESH
        )
    pl.semaphore_signal(barrier, inc=1, device_id=pair, device_id_type=MESH)

    wall[pl.ds(pl.multiple_of(place * rows, 16), rows), :] = weights_ref[...].astype(BF16)
    dout_all[pl.ds(pl.multiple_of(y * tokens, 16), tokens), :] = dout_ref[...]
    pl.semaphore_wait(barrier, RING)

    def pair_copy(source, target, slot):
        return pltpu.make_async_remote_copy(
            src_ref=source,
            dst_ref=target,
            send_sem=send_sem.at[slot],
            recv_sem=recv_sem.at[slot],
            device_id=pair,
            device_id_type=MESH,
        )

    def w_view(z, half):
        start = (y * 2 + z) * rows + half * (rows // 2)
        return wall.at[pl.ds(pl.multiple_of(start, 16), rows // 2), :]

    own = Gather(wall, rows, lambda s: (s * 2 + zh) * rows, send_sem, recv_sem, W_OWN, y, column)
    other = Gather(
        wall, rows, lambda s: (s * 2 + (1 - zh)) * rows, send_sem, recv_sem, W_PAIR, y, column
    )
    douts = Gather(dout_all, tokens, lambda s: s * tokens, send_sem, recv_sem, DOUT, y, column)

    tile = 128
    tiles = width // tile
    turned = 0

    def turn(until):
        nonlocal turned
        until = min(until, tiles)
        if until <= turned:
            return

        @pl.loop(turned, until)
        def _(t):
            at = pl.multiple_of(t * tile, tile)
            acts_t[pl.ds(at, tile), :] = acts[:, pl.ds(at, tile)].T

        turned = until

    for half in range(2):
        pair_copy(w_view(zh, half), w_view(zh, half), Z_W + half).start()
    own.start()
    douts.start()
    acts_copy.wait()
    turn(3)
    own.relay(1)
    turn(6)
    douts.relay(1)
    turn(9)
    for half in range(2):
        pair_copy(w_view(zh, half), w_view(1 - zh, half), Z_W + half).wait_recv()
    other.start()
    own.relay(2)
    turn(14)
    other.relay(1)
    douts.relay(2)
    turn(19)
    own.relay(3)
    turn(24)
    other.relay(2)
    douts.relay(3)
    turn(30)
    own.relay(4)
    other.relay(3)
    turn(tiles)
    douts.relay(4)
    other.relay(4)

    near_cos, near_sin = near_ref[0], near_ref[1]
    far_cos = far_ref[0, pl.ds(place, 1), :]
    far_sin = far_ref[1, pl.ds(place, 1), :]
    cosine = near_cos * far_cos - near_sin * far_sin
    sine = near_sin * far_cos + near_cos * far_sin
    half_head = head // 2
    lane = lax.broadcasted_iota(jnp.int32, (tokens, head), 1)
    signed = jnp.where(lane < half_head, -sine, sine)

    def turned_by(matrix, direction):
        return matrix * cosine + direction * pltpu.roll(matrix, half_head, 1) * signed

    proj = dot_nn(acts[...], wall[...]) * pscale
    here = pl.ds(pl.multiple_of(y * tokens, 16), tokens)
    mine = pl.ds(pl.multiple_of(zh * tokens, 16), tokens)
    query_all[here, :] = turned_by(proj[:, :head], 1.0).astype(BF16)
    queries = Gather(
        query_all, tokens, lambda s: s * tokens, send_sem, recv_sem, QUERY, y, column
    )
    queries.start()
    kv_all[mine, :head] = turned_by(proj[:, head : 2 * head], 1.0).astype(BF16)
    kv_all[mine, head:] = proj[:, 2 * head :].astype(BF16)
    theirs = pl.ds(pl.multiple_of((1 - zh) * tokens, 16), tokens)
    pair_copy(kv_all.at[mine, :], kv_all.at[mine, :], Z_KV).start()
    stats_own[...] = jnp.zeros_like(stats_own)
    for hop in range(1, RING // 2 + 1):
        queries.relay(hop)
    pair_copy(kv_all.at[mine, :], kv_all.at[theirs, :], Z_KV).wait_recv()

    sub = min(128, 2 * tokens)

    @pl.loop(y, RING)
    def _(block):
        at = pl.ds(pl.multiple_of(block * tokens, 16), tokens)
        query = query_all[at, :]
        dout = dout_all[at, :]
        total = jnp.zeros((1, tokens), F32)
        cross = jnp.zeros((1, tokens), F32)
        for part in range(0, 2 * tokens, sub):
            score = dot_nt(kv_all[part : part + sub, :head], query)
            dprob = dot_nt(kv_all[part : part + sub, head:], dout)
            tangent = jnp.tanh(score * (qscale / SOFT_CAP))
            key_at = lax.broadcasted_iota(jnp.int32, (sub, tokens), 0) + part
            query_at = lax.broadcasted_iota(jnp.int32, (sub, tokens), 1)
            keep = key_at - query_at <= (block - y) * (2 * tokens) + zh * tokens
            expo = jnp.where(keep, jnp.exp(SOFT_CAP * tangent), 0.0)
            expo_buf[block, part : part + sub, :] = expo
            slope_buf[block, part : part + sub, :] = expo * (1.0 - tangent * tangent)
            dprob_buf[block, part : part + sub, :] = dprob
            total += jnp.sum(expo, axis=0, keepdims=True)
            cross += jnp.sum(expo * dprob, axis=0, keepdims=True)
        stats_own[pl.ds(block, 1), :] = total
        stats_own[pl.ds(block + RING, 1), :] = cross

    def stats_copy(ahead):
        return pltpu.make_async_remote_copy(
            src_ref=stats_own,
            dst_ref=stats_in.at[ahead],
            send_sem=send_sem.at[STATS + ahead],
            recv_sem=recv_sem.at[STATS + ahead],
            device_id=column(lax.rem(y + ahead, RING)),
            device_id_type=MESH,
        )

    for ahead in range(1, RING):
        stats_copy(ahead).start()
    dq_buf[...] = jnp.zeros_like(dq_buf)
    dkv_acc[...] = jnp.zeros_like(dkv_acc)
    stats = stats_own[...]
    for ahead in range(1, RING):
        stats_copy(ahead).wait_recv()
        stats += stats_in[ahead]
    for ahead in range(1, RING):
        stats_copy(ahead).wait_send()
    inverse = 1.0 / stats[:RING, :]
    stats_own[:RING, :] = inverse
    stats_own[RING:, :] = stats[RING:, :] * inverse

    @pl.loop(y, RING)
    def _(block):
        at = pl.ds(pl.multiple_of(block * tokens, 16), tokens)
        query = query_all[at, :]
        dout = dout_all[at, :]
        inv = stats_own[pl.ds(block, 1), :]
        delta = stats_own[pl.ds(block + RING, 1), :]
        dquery = jnp.zeros((tokens, head), F32)
        for part in range(0, 2 * tokens, sub):
            span = slice(part, part + sub)
            prob = (expo_buf[block, span, :] * inv).astype(BF16)
            dscore = (
                slope_buf[block, span, :] * (dprob_buf[block, span, :] - delta) * (inv * qscale)
            ).astype(BF16)
            dkv_acc[span, :head] += dot_nn(dscore, query)
            dkv_acc[span, head:] += dot_nn(prob, dout)
            dquery += dot_tn(dscore, kv_all[span, :head])
        dq_buf[at, :] = dquery

    dkv_out[...] = dkv_acc[theirs, :].astype(BF16)
    dkv_copy = pair_copy(dkv_out, dkv_in, Z_DKV)
    dkv_copy.start()

    def dq_own(target, half):
        start = target * tokens + half * (tokens // 2)
        return dq_buf[pl.ds(pl.multiple_of(start, 16), tokens // 2), :]

    dqueries = Scatter(dq_own, dq_out, dq_in, send_sem, recv_sem, DQUERY, y, column)
    for step in range(RING // 2):
        dqueries.step(step)
    dkv_copy.wait_recv()
    dkv = dkv_acc[mine, :] + dkv_in[...].astype(F32)
    dproj[:, head : 2 * head] = turned_by(dkv[:, :head], -1.0).astype(BF16)
    dproj[:, 2 * head :] = dkv[:, head:].astype(BF16)
    dquery = jnp.concatenate([dqueries.result(0), dqueries.result(1)], axis=0)
    dproj[:, :head] = turned_by(dquery, -1.0).astype(BF16)

    def g_term(z):
        def term(target, half):
            start = (target * 2 + z) * rows + half * (rows // 2)
            block = acts_t[pl.ds(pl.multiple_of(start, 16), rows // 2), :]
            return dot_nn(block, dproj[...]) * pscale

        return term

    g_pair = Scatter(
        g_term(1 - zh), g_out_pair, g_in_pair, send_sem, recv_sem, G_PAIR, y, column
    )
    g_own = Scatter(g_term(zh), g_out_own, g_in_own, send_sem, recv_sem, G_OWN, y, column)
    g_pair.step(0)
    g_pair.step(1)
    g_own.step(0)
    g_pair.step(2)
    g_own.step(1)
    g_pair.step(3)
    g_own.step(2)
    for half in range(2):
        z_out[half] = g_pair.result(half).astype(BF16)
        pair_copy(z_out.at[half], z_in.at[half], Z_G + half).start()
    g_own.step(3)
    momentum_copy.wait()
    for half in range(2):
        grad = g_own.result(half)
        pair_copy(z_out.at[half], z_in.at[half], Z_G + half).wait_recv()
        grad += z_in[half].astype(F32)
        span = slice(half * (rows // 2), (half + 1) * (rows // 2))
        moved = MOMENTUM_DECAY * momentum[span, :] + grad
        new_momentum_ref[span, :] = moved
        stepped_ref[span, :] = weights_ref[span, :] - LEARNING_RATE * moved

    for gather in (own, other, douts, queries):
        gather.drain()
    for scatter in (dqueries, g_pair, g_own):
        scatter.drain()
    for half in range(2):
        pair_copy(w_view(zh, half), w_view(zh, half), Z_W + half).wait_send()
        pair_copy(z_out.at[half], z_in.at[half], Z_G + half).wait_send()
    pair_copy(kv_all.at[mine, :], kv_all.at[mine, :], Z_KV).wait_send()
    dkv_copy.wait_send()


def rope_tables(tokens, places, head):
    half = head // 2
    freqs = ROPE_BASE ** (-(np.arange(half, dtype=np.float64) * 2.0 / head))
    freqs = np.concatenate([freqs, freqs])
    near = np.arange(tokens, dtype=np.float64)[:, None] * freqs
    far = (np.arange(places, dtype=np.float64) * tokens)[:, None] * freqs
    return (
        np.stack([np.cos(near), np.sin(near)]).astype(np.float32),
        np.stack([np.cos(far), np.sin(far)]).astype(np.float32),
    )


def passed_along(value, axis, steps):
    count = lax.axis_size(axis)
    pairs = [(source, (source + steps) % count) for source in range(count)]
    return lax.ppermute(value, axis, pairs)


def on_device(activations, weights, momentum, cotangent, step):
    acts = activations[0]
    params = weights[0]
    moment = momentum[0]
    dout = cotangent[0]
    tokens, width = acts.shape
    rows, columns = params.shape
    head = dout.shape[1]
    places = lax.axis_size("fsdp")
    near, far = rope_tables(tokens, places, head)
    vmem = pl.BlockSpec(memory_space=pltpu.VMEM)
    anywhere = pl.BlockSpec(memory_space=pl.ANY)
    steps = 16
    new_moment, stepped = pl.pallas_call(
        kernel,
        out_shape=[jax.ShapeDtypeStruct((rows, columns), F32)] * 2,
        in_specs=[anywhere, vmem, anywhere, vmem, vmem, vmem],
        out_specs=[vmem, vmem],
        scratch_shapes=[
            pltpu.VMEM((tokens, width), BF16),
            pltpu.VMEM((width, tokens), BF16),
            pltpu.VMEM((rows, columns), F32),
            pltpu.VMEM((width, columns), BF16),
            pltpu.VMEM((RING * tokens, head), BF16),
            pltpu.VMEM((RING * tokens, head), BF16),
            pltpu.VMEM((2 * tokens, 2 * head), BF16),
            pltpu.VMEM((RING, 2 * tokens, tokens), F32),
            pltpu.VMEM((RING, 2 * tokens, tokens), F32),
            pltpu.VMEM((RING, 2 * tokens, tokens), F32),
            pltpu.VMEM((2 * RING, tokens), F32),
            pltpu.VMEM((RING, 2 * RING, tokens), F32),
            pltpu.VMEM((RING * tokens, head), F32),
            pltpu.VMEM((steps, tokens // 2, head), BF16),
            pltpu.VMEM((steps, tokens // 2, head), BF16),
            pltpu.VMEM((2 * tokens, 2 * head), F32),
            pltpu.VMEM((tokens, 2 * head), BF16),
            pltpu.VMEM((tokens, 2 * head), BF16),
            pltpu.VMEM((tokens, columns), BF16),
            pltpu.VMEM((steps, rows // 2, columns), BF16),
            pltpu.VMEM((steps, rows // 2, columns), BF16),
            pltpu.VMEM((steps, rows // 2, columns), BF16),
            pltpu.VMEM((steps, rows // 2, columns), BF16),
            pltpu.VMEM((2, rows // 2, columns), BF16),
            pltpu.VMEM((2, rows // 2, columns), BF16),
            pltpu.SemaphoreType.DMA((SEMS,)),
            pltpu.SemaphoreType.DMA((SEMS,)),
            pltpu.SemaphoreType.DMA((2,)),
        ],
        compiler_params=pltpu.CompilerParams(
            collective_id=0, has_side_effects=True, vmem_limit_bytes=56 * 2**20
        ),
        name="attention_step",
    )(acts, params, moment, dout, jnp.asarray(near), jnp.asarray(far))
    replicas = lax.axis_size("rep")
    branches = [
        functools.partial(
            lambda by, value: passed_along(value.astype(BF16), "rep", by).astype(F32),
            2**level % replicas,
        )
        for level in range(PERIOD)
    ]
    partner = lax.switch(step[0] % PERIOD, branches, stepped)
    new_weights = (stepped + partner) * 0.5
    return (new_weights[None], new_moment[None])


def solution(mesh):
    spec = P("rep", "fsdp", None)
    return jax.shard_map(
        on_device,
        mesh=mesh,
        in_specs=(spec, spec, spec, spec, P()),
        out_specs=(spec, spec),
        check_vma=False,
    )
```

time: 776 us -> 148 us (0.19)
  waiting for transfers between devices: 613 us -> 8.1 us
  Pallas kernels: 0 us -> 128 us
  blocking collectives: 93.6 us -> 0 us
  matrix products: 34.1 us -> 0 us
  between operations: 14.9 us -> 1.32 us
  other arithmetic: 10.1 us -> 0.87 us
    all_gather x5 -> x0, waiting for transfers between devices: 372 us -> none  [the longest x1 132 us: on_device(): lax.all_gather(params.astype(jnp.bfloat16), 'fsdp', axis=0, tiled=True)]
    reduce_scatter x1 -> x0, waiting for transfers between devices: 232 us -> none  [on_device(): lax.psum_scatter((inner_first(columns, dproj) * float(width) ** (-0.5)).a...]
    pallas_call x0 -> x1, Pallas kernels: none -> 128 us  [on_device(): pl.pallas_call(kernel, out_shape=[jax.ShapeDtypeStruct((rows, columns), F...]
    all_gather x2 -> x0, blocking collectives: 93.6 us -> none  [the longest x1 51.7 us: on_device(): lax.all_gather(row_total.astype(jnp.bfloat16), 'fsdp', axis=0, tiled=True)]
    dot_general x8 -> x0, matrix products: 34.1 us -> none  [the longest x3 13.2 us: inner_first(): lax.dot_general(left, right, (((0,), (0,)), ((), ())), preferred_element_...]
  transfers between devices with their start and end apart: 7 -> 1, of which waited for: 6 -> 1; matrix products, arithmetic and copies ran while one was open for 3% -> 0% of each run, Pallas kernels for 0% -> 0%
where the time goes in v1:
time: 148 us; the launch traced here: 147 us
  Pallas kernels  128 us (86%)
  starting transfers between devices  8.65 us (6%)
  waiting for transfers between devices  8.1 us (5%)
    pallas_call x1, Pallas kernels, on_device(): pl.pallas_call(kernel, out_shape=[jax.ShapeDtypeStruct((rows, columns), F...  128 us
    ppermute x1, starting transfers between devices, passed_along(): return lax.ppermute(value, axis, pairs)  8.65 us
    ppermute x1, waiting for transfers between devices, passed_along(): return lax.ppermute(value, axis, pairs)  8.1 us
  transfers between devices with their start and end apart: 1, of which 1 were waited for; matrix products, arithmetic and copies ran while one was open for 0% of the time, Pallas kernels for 0%

profile of v1, /device:TPU:16, one launch (start us, length us, event | category | flops | bytes accessed | tf_op | source)
XLA Modules:
  0.0 147.4 jit_solution(56029117140805856)
XLA Ops:
  1.3 127.7 %attention_step.1 = (f32[288,384]{1,0:T(8,128)}, f32[288,384]{1,0:T(8,128)S(1)}) custom-call(bf16[256,4608]{1,0:T(8,128)(2,1)} %bitcast.11, f32[288,384]{1,0:T(8,128)} %bitcast.12, f32[288,384]{1,0:T(8,128)} %bitcast.13, bf16[256,128]{1,0:T(8,128)(2,1)} %bitcast.15, f32[2,256,128]{2,1,0:T(8,128)} %constant.21.clone.near_ref, ...), custom_call_target="tpu_custom_call" | custom-call | tf_op jit(solution)/shard_map/attention_step/pallas_call | solution.py:460
  129.0 0.0 copy-start
  129.0 16.9 %conditional.4 = (f32[288,384]{1,0:T(8,128)S(1)}) conditional(s32[]{:T(128)} %clamp.3, f32[288,384]{1,0:T(8,128)S(1)} %get-tuple-element.19, f32[288,384]{1,0:T(8,128)S(1)} %get-tuple-element.19, f32[288,384]{1,0:T(8,128)S(1)} %get-tuple-element.19, f32[288,384]{1,0:T(8,128)S(1)} %get-tuple-element.19), branch_computations={%region_0.1_spmd, %region_1.2_spmd, %region_2.3_spmd, %region_3.4_... | conditional | flops 221184 | bytes 2211888
  129.1 8.6 %collective-permute-start.2 = (bf16[288,384]{1,0:T(8,128)(2,1)S(1)}, bf16[288,384]{1,0:T(8,128)(2,1)S(1)}, u32[]{:S(2)}, u32[]{:S(2)}) collective-permute-start(bf16[288,384]{1,0:T(8,128)(2,1)S(1)} %convert_element_type.30), channel_id=1, source_target_pairs={{0,64},{16,80},{32,96},{48,112},{64,128},{80,144},{96,160},{112,17... | collective-permute-start | bytes 663560 | tf_op jit(solution)/shard_map/cond/branch_2_fun/ppermute | solution.py:444
  137.7 8.1 %collective-permute-done.2 = bf16[288,384]{1,0:T(8,128)(2,1)S(1)} collective-permute-done((bf16[288,384]{1,0:T(8,128)(2,1)S(1)}, bf16[288,384]{1,0:T(8,128)(2,1)S(1)}, u32[]{:S(2)}, u32[]{:S(2)}) %collective-permute-start.2) | collective-permute-done | bytes 221216 | tf_op jit(solution)/shard_map/cond/branch_2_fun/ppermute | solution.py:444
  145.9 0.8 multiply_bitcast_fusion
  146.7 0.0 copy-done
  146.7 0.8 copy.15
  (2 shorter events, 0.1 us)
Async XLA Ops:
  129.0 17.7 %copy-start = (f32[288,384]{1,0:T(8,128)S(1)}, f32[288,384]{1,0:T(8,128)}, u32[]{:S(2)}) copy-start(f32[288,384]{1,0:T(8,128)} %get-tuple-element.20) | copy-start | bytes 1327108
  129.1 16.8 %collective-permute-start.2 = (bf16[288,384]{1,0:T(8,128)(2,1)S(1)}, bf16[288,384]{1,0:T(8,128)(2,1)S(1)}, u32[]{:S(2)}, u32[]{:S(2)}) collective-permute-start(bf16[288,384]{1,0:T(8,128)(2,1)S(1)} %convert_element_type.30), channel_id=1, source_target_pairs={{0,64},{16,80},{32,96},{48,112},{64,128},{80,144},{96,160},{112,17... | collective-permute-start | bytes 663560 | tf_op jit(solution)/shard_map/cond/branch_2_fun/ppermute | solution.py:444

commit v2 on v0

v2 whole, which is shorter than its diff:
```python
import functools

import jax
import jax.numpy as jnp
import numpy as np
from jax import lax
from jax.experimental import pallas as pl
from jax.experimental.pallas import tpu as pltpu
from jax.sharding import PartitionSpec as P

HEADS = 32
PERIOD = 4
SOFT_CAP = 50.0
ROPE_BASE = 10000.0
MOMENTUM_DECAY = 0.9
LEARNING_RATE = 0.5
RING = 8
FAR = RING // 2
BF16 = jnp.bfloat16
F32 = jnp.float32
MESH = pl.DeviceIdType.MESH
SEMS = 192
OFFSETS = (4, 3, 5, 2, 6, 1, 7, 0)
GROUPS = ((0, 3), (3, 5), (5, 8))

GATHER_ORDER = (
    1, 27, 0, 91, 99, 51, 2, 101, 94, 92, 93, 50, 97, 52, 26, 100, 103, 102, 96, 95,
    75, 76, 98, 25, 3, 29, 19, 9, 4, 17, 28, 18, 10, 67, 69, 59, 54, 42, 34, 20,
    35, 46, 11, 21, 6, 68, 5, 45, 12, 43, 61, 71, 60, 44, 36, 37, 13, 31, 23, 53,
    22, 14, 7, 8, 30, 62, 15, 56, 38, 48, 70, 33, 55, 16, 24, 39, 63, 47, 64, 77,
    73, 58, 32, 49, 78, 40, 104, 85, 41, 72, 86, 74, 65, 57, 66, 79, 80, 105, 106, 83,
    84, 89, 88, 107, 108, 87, 90, 81, 82,
)
SCATTER_ORDER = (
    3, 2, 77, 1, 0, 7, 6, 8, 11, 12, 23, 16, 15, 13, 9, 33, 5, 4, 34, 35,
    38, 45, 18, 37, 36, 17, 24, 25, 14, 46, 10, 40, 55, 60, 59, 20, 56, 39, 26, 67,
    57, 19, 48, 27, 58, 62, 61, 42, 41, 68, 21, 22, 47, 28, 63, 64, 69, 70, 31, 43,
    44, 49, 50, 65, 66, 71, 72, 53, 29, 30, 51, 52, 75, 73, 74, 32, 54, 76,
)


def dot_nn(left, right):
    return lax.dot_general(left, right, (((1,), (0,)), ((), ())), preferred_element_type=F32)


def dot_nt(left, right):
    return lax.dot_general(left, right, (((1,), (1,)), ((), ())), preferred_element_type=F32)


def dot_tn(left, right):
    return lax.dot_general(left, right, (((0,), (0,)), ((), ())), preferred_element_type=F32)


def aligned(start):
    return start if isinstance(start, int) else pl.multiple_of(start, 16)


class Transfers:
    def __init__(self, send_sem, recv_sem):
        self.send_sem, self.recv_sem = send_sem, recv_sem
        self.slots, self.made, self.waited, self.started = {}, {}, set(), []

    def declare(self, name, source, target, landed, device):
        slot = self.slots.setdefault(name, len(self.slots))

        def descriptor(dst):
            return pltpu.make_async_remote_copy(
                src_ref=source(),
                dst_ref=dst(),
                send_sem=self.send_sem.at[slot],
                recv_sem=self.recv_sem.at[slot],
                device_id=device,
                device_id_type=MESH,
            )

        self.made[name] = (descriptor, target, landed)

    def start(self, name):
        descriptor, target, _ = self.made[name]
        descriptor(target).start()
        self.started.append(name)

    def arrived(self, name):
        if name not in self.waited:
            self.waited.add(name)
            descriptor, _, landed = self.made[name]
            descriptor(landed).wait_recv()

    def drain(self):
        for name in self.started:
            descriptor, target, _ = self.made[name]
            descriptor(target).wait_send()


class Plan:
    def __init__(self, transfers):
        self.transfers = transfers
        self.tasks = []

    def send(self, name, link, load, needs=(), prepare=None, cost=0.0):
        self.tasks.append((name, link, load, tuple(needs), prepare, cost))

    def compute(self, name, cost, needs, emit):
        self.tasks.append((name, None, 0, tuple(needs), emit, cost))

    def run(self, order):
        for at in order:
            name, link, _, needs, emit, _ = self.tasks[at]
            for need in needs:
                if need in self.transfers.made:
                    self.transfers.arrived(need)
            if emit is not None:
                emit()
            if link is not None:
                self.transfers.start(name)


def kernel(
    acts_hbm,
    weights_ref,
    momentum_hbm,
    dout_ref,
    near_ref,
    far_ref,
    grad_ref,
    stepped_ref,
    acts,
    acts_t,
    momentum,
    wall,
    dout_all,
    query_all,
    keys,
    values,
    expo_buf,
    slope_buf,
    dprob_buf,
    sums_own,
    sums_in,
    inv_buf,
    delta_buf,
    dq_buf,
    dq_out,
    dq_in,
    dk_acc,
    dv_acc,
    dkv_out,
    dkv_in,
    dproj,
    own_out,
    own_in,
    pair_out,
    pair_in,
    share_out,
    share_in,
    z_out,
    z_in,
    terms,
    send_sem,
    recv_sem,
    local_sem,
):
    rows = weights_ref.shape[0]
    tokens, head = dout_ref.shape
    width = acts.shape[1]
    share = rows // 9 * 2
    kept = rows - share
    qscale = float(width // HEADS) ** (-0.5)
    pscale = float(width) ** (-0.5)
    rep = lax.axis_index("rep")
    place = lax.axis_index("fsdp")
    y = lax.div(place, 2)
    zh = lax.rem(place, 2)

    def around(step):
        return lax.rem(y + step % RING, RING)

    def column(step):
        return (rep, around(step) * 2 + zh)

    pair = (rep, y * 2 + (1 - zh))

    acts_copy = pltpu.make_async_copy(acts_hbm, acts, local_sem.at[0])
    acts_copy.start()
    momentum_copy = pltpu.make_async_copy(momentum_hbm, momentum, local_sem.at[1])
    momentum_copy.start()

    barrier = pltpu.get_barrier_semaphore()
    greeted = [column(step) for step in range(1, RING)] + [pair]
    for device in greeted:
        pl.semaphore_signal(barrier, inc=1, device_id=device, device_id_type=MESH)
    for part in range(3):
        wall[part, pl.ds(aligned(place * rows), rows), :] = weights_ref[
            :, part * head : (part + 1) * head
        ].astype(BF16)
    dout_all[pl.ds(aligned(y * tokens), tokens), :] = dout_ref[...]
    pl.semaphore_wait(barrier, len(greeted))

    moves = Transfers(send_sem, recv_sem)
    ways = ((0, 1, "up"), (1, -1, "down"))

    def gather(plan, tag, view, count, needs_of, strides=False):
        for hop in range(1, FAR + 1):
            for way, sign, link in ways:
                low, high = 0, count
                if hop == FAR:
                    low, high = ((0, count // 2), (count // 2, count))[way]
                name = (tag, hop, way)
                jump = 2 if strides and hop % 2 == 0 else 1
                held = hop - jump
                moves.declare(
                    name,
                    functools.partial(view, -sign * held, low, high),
                    functools.partial(view, -sign * held, low, high),
                    functools.partial(view, -sign * hop, low, high),
                    column(sign * jump),
                )
                needs = [(tag, held, way)] if held else needs_of
                plan.send(name, link, jump * (high - low) * head * 2, needs)

    def hops(tag):
        return [(tag, hop, way) for hop in range(1, FAR + 1) for way in range(2)]

    plan = Plan(moves)

    def wall_view(part, z, step, low, high):
        start = (around(step) * 2 + z) * rows + low
        return wall.at[part, pl.ds(aligned(start), high - low), :]

    arrivals = []
    for part in range(3):
        mine = functools.partial(wall_view, part, zh)
        theirs = functools.partial(wall_view, part, 1 - zh)
        first = ("first", part)
        moves.declare(
            first,
            functools.partial(mine, 0, 0, kept),
            functools.partial(mine, 0, 0, kept),
            functools.partial(theirs, 0, 0, kept),
            pair,
        )
        plan.send(first, "z", kept * head * 2)
        gather(plan, ("own", part), mine, rows, ())
        gather(plan, ("pair", part), theirs, kept, [first])
        names = hops(("own", part)) + hops(("pair", part)) + [first]
        passed = [(0, 0, 0)] + [
            (-sign * hop, hop, way)
            for hop in range(1, FAR + 1)
            for way, sign, _ in ways
            if hop < FAR or way == 1
        ]
        for step, hop, way in passed:
            name = ("share", part, step)
            moves.declare(
                name,
                functools.partial(mine, step, kept, rows),
                functools.partial(mine, step, kept, rows),
                functools.partial(theirs, step, kept, rows),
                pair,
            )
            needs = [] if hop == 0 else [(("own", part), hop, way)]
            plan.send(name, "z", share * head * 2, needs)
            names.append(name)
        arrivals.append(names)

    def block_view(buffer, step, low, high):
        return buffer.at[pl.ds(aligned(around(step) * tokens + low), high - low), :]

    gather(plan, "dout", functools.partial(block_view, dout_all), tokens, ())
    gather(plan, "query", functools.partial(block_view, query_all), tokens, ["query"], True)

    half_head = head // 2
    far_cos = far_ref[0, pl.ds(place, 1), :]
    far_sin = far_ref[1, pl.ds(place, 1), :]

    def turned_by(matrix, direction):
        near_cos, near_sin = near_ref[0], near_ref[1]
        cosine = near_cos * far_cos - near_sin * far_sin
        sine = near_sin * far_cos + near_cos * far_sin
        lane = lax.broadcasted_iota(jnp.int32, (tokens, head), 1)
        signed = jnp.where(lane < half_head, -sine, sine)
        return matrix * cosine + direction * pltpu.roll(matrix, half_head, 1) * signed

    here = pl.ds(aligned(y * tokens), tokens)
    mine_rows = pl.ds(aligned(zh * tokens), tokens)
    their_rows = pl.ds(aligned((1 - zh) * tokens), tokens)

    def projected(part):
        return dot_nn(acts[...], wall[part]) * pscale

    def make_query():
        query_all[here, :] = turned_by(projected(0), 1.0).astype(BF16)

    def make_keys():
        keys[mine_rows, :] = turned_by(projected(1), 1.0).astype(BF16)

    def make_values():
        values[mine_rows, :] = projected(2).astype(BF16)

    tile = 128
    tiles = width // tile
    turns = 12

    def turn(at):
        @pl.loop(at * tiles // turns, (at + 1) * tiles // turns)
        def _(t):
            at = pl.multiple_of(t * tile, tile)
            acts_t[pl.ds(at, tile), :] = acts[:, pl.ds(at, tile)].T

    plan.compute("acts", 0.1, (), acts_copy.wait)
    for at in range(turns):
        plan.compute(("turn", at), 0.25, ["acts"], functools.partial(turn, at))
    plan.compute("query", 1.0, arrivals[0] + ["acts"], make_query)
    for tag, buffer, made in (("keys", keys, make_keys), ("values", values, make_values)):
        part = 1 if tag == "keys" else 2
        plan.compute(tag, 0.9, arrivals[part] + ["acts"], made)
        moves.declare(
            (tag, "z"),
            functools.partial(lambda ref: ref.at[mine_rows, :], buffer),
            functools.partial(lambda ref: ref.at[mine_rows, :], buffer),
            functools.partial(lambda ref: ref.at[their_rows, :], buffer),
            pair,
        )
        plan.send((tag, "z"), "z", tokens * head * 2, [tag])
    plan.run(GATHER_ORDER)

    for name in hops("query") + [("keys", "z")]:
        moves.arrived(name)
    sub = min(128, 2 * tokens)
    sums_own[...] = jnp.zeros_like(sums_own)

    @pl.loop(y, RING)
    def _(block):
        query = query_all[pl.ds(aligned(block * tokens), tokens), :]
        total = jnp.zeros((1, tokens), F32)
        for low in range(0, 2 * tokens, sub):
            span = slice(low, low + sub)
            score = dot_nt(keys[span, :], query)
            tangent = jnp.tanh(score * (qscale / SOFT_CAP))
            key_at = lax.broadcasted_iota(jnp.int32, (sub, tokens), 0) + low
            query_at = lax.broadcasted_iota(jnp.int32, (sub, tokens), 1)
            keep = key_at - query_at <= (block - y) * (2 * tokens) + zh * tokens
            expo = jnp.where(keep, jnp.exp(SOFT_CAP * tangent), 0.0)
            expo_buf[block, span, :] = expo
            slope_buf[block, span, :] = expo * (1.0 - tangent * tangent)
            total += jnp.sum(expo, axis=0, keepdims=True)
        sums_own[0, pl.ds(block, 1), :] = total

    def exchange(kind):
        for step in range(1, RING):
            name = ("sums", kind, step)
            moves.declare(
                name,
                lambda: sums_own.at[kind],
                functools.partial(lambda at: sums_in.at[kind, at], step),
                functools.partial(lambda at: sums_in.at[kind, at], step),
                column(step),
            )
            moves.start(name)

    def summed(kind):
        total = sums_own[kind]
        for step in range(1, RING):
            moves.arrived(("sums", kind, step))
            total += sums_in[kind, step]
        return total

    exchange(0)
    for name in hops("dout") + [("values", "z")]:
        moves.arrived(name)

    @pl.loop(y, RING)
    def _(block):
        dout = dout_all[pl.ds(aligned(block * tokens), tokens), :]
        cross = jnp.zeros((1, tokens), F32)
        for low in range(0, 2 * tokens, sub):
            span = slice(low, low + sub)
            dprob = dot_nt(values[span, :], dout)
            dprob_buf[block, span, :] = dprob
            cross += jnp.sum(expo_buf[block, span, :] * dprob, axis=0, keepdims=True)
        sums_own[1, pl.ds(block, 1), :] = cross

    exchange(1)
    dq_buf[...] = jnp.zeros_like(dq_buf)
    dk_acc[...] = jnp.zeros_like(dk_acc)
    dv_acc[...] = jnp.zeros_like(dv_acc)
    inverse = 1.0 / summed(0)
    inv_buf[...] = inverse

    @pl.loop(y, RING)
    def _(block):
        dout = dout_all[pl.ds(aligned(block * tokens), tokens), :]
        inv = inv_buf[pl.ds(block, 1), :]
        for low in range(0, 2 * tokens, sub):
            span = slice(low, low + sub)
            dv_acc[span, :] += dot_nn((expo_buf[block, span, :] * inv).astype(BF16), dout)

    def swap(kind, acc):
        dkv_out[kind] = acc[their_rows, :].astype(BF16)
        moves.declare(
            ("swap", kind),
            lambda: dkv_out.at[kind],
            lambda: dkv_in.at[kind],
            lambda: dkv_in.at[kind],
            pair,
        )
        moves.start(("swap", kind))

    swap(1, dv_acc)
    delta_buf[...] = summed(1) * inverse

    @pl.loop(y, RING)
    def _(block):
        at = pl.ds(aligned(block * tokens), tokens)
        query = query_all[at, :]
        inv = inv_buf[pl.ds(block, 1), :] * qscale
        delta = delta_buf[pl.ds(block, 1), :]
        dquery = jnp.zeros((tokens, head), F32)
        for low in range(0, 2 * tokens, sub):
            span = slice(low, low + sub)
            dscore = slope_buf[block, span, :] * (dprob_buf[block, span, :] - delta) * inv
            dscore = dscore.astype(BF16)
            dk_acc[span, :] += dot_nn(dscore, query)
            dquery += dot_tn(dscore, keys[span, :])
        dq_buf[at, :] = dquery

    swap(0, dk_acc)

    plan = Plan(moves)

    def pieces(low, high, value, added, store):
        edges = {low, high}
        for ref, start, stop in added:
            edges |= {edge for edge in (start, stop) if low < edge < high}
        edges = sorted(edges)
        for start, stop in zip(edges[:-1], edges[1:]):
            total = value[start - low : stop - low]
            for ref, first, last in added:
                if first <= start and stop <= last:
                    total += ref[start - first : stop - first, :].astype(F32)
            store(start, stop, total)

    def chain(tag, term, extra, outgoing, incoming, count, needs_of, strides=False):
        for step in range(FAR):
            for way, sign, link in ways:
                half = ((0, count // 2), (count // 2, count))[way]
                low, high = half if step == 0 else (0, count)
                name = (tag, step, way)
                offset = (sign * (FAR - step)) % RING
                jump = 2 if strides and step % 2 == 0 else 1
                if strides:
                    inputs = [0, 1] if step == 2 else []
                else:
                    inputs = [step - 1] if step else []

                def prepare(
                    step=step, way=way, low=low, high=high, offset=offset, inputs=inputs, half=half
                ):
                    added = list(extra(offset))
                    for earlier in inputs:
                        first, last = (0, count) if earlier else half
                        added.append((incoming.at[earlier, way], first, last))

                    def store(start, stop, total):
                        outgoing[step, way, start - low : stop - low, :] = total.astype(BF16)

                    pieces(low, high, term(offset, low, high), added, store)

                def view(ref, step=step, way=way, size=high - low):
                    return ref.at[step, way, pl.ds(0, size), :]

                moves.declare(
                    name,
                    functools.partial(view, outgoing),
                    functools.partial(view, incoming),
                    functools.partial(view, incoming),
                    column(sign * jump),
                )
                needs = list(needs_of(offset, low, high))
                needs += [(tag, earlier, way) for earlier in inputs]
                plan.send(name, link, jump * (high - low) * head * 2, needs, prepare, 0.1)

    def last_hops(tag):
        return [(tag, FAR - 1, way) for way in range(2)]

    def dq_term(offset, low, high):
        start = around(offset) * tokens + low
        return dq_buf[pl.ds(aligned(start), high - low), :]

    chain(
        "dquery",
        dq_term,
        lambda offset: (),
        dq_out,
        dq_in,
        tokens,
        lambda *a: (),
        True,
    )

    def finish_dv():
        dproj[2] = (dv_acc[mine_rows, :] + dkv_in[1].astype(F32)).astype(BF16)

    def finish_dk():
        total = dk_acc[mine_rows, :] + dkv_in[0].astype(F32)
        dproj[1] = turned_by(total, -1.0).astype(BF16)

    def finish_dq():
        total = dq_buf[here, :]
        for way in range(2):
            total += dq_in[2, way].astype(F32) + dq_in[3, way].astype(F32)
        dproj[0] = turned_by(total, -1.0).astype(BF16)

    plan.compute(("dproj", 2), 0.2, [("swap", 1)], finish_dv)
    plan.compute(("dproj", 1), 0.3, [("swap", 0)], finish_dk)
    plan.compute(("dproj", 0), 0.4, [("dquery", step, way) for step in (2, 3) for way in range(2)], finish_dq)

    for part in (2, 1, 0):
        ready = ("terms", part)

        def multiply(part=part):
            size = width // 9

            @pl.loop(0, 9)
            def _(at):
                span = pl.ds(pl.multiple_of(at * size, 16), size)
                terms[part, span, :] = dot_nn(acts_t[span, :], dproj[part]) * pscale

        plan.compute(ready, 0.8, [("dproj", part)], multiply)

        def term(z, offset, low, high, part=part):
            start = (around(offset) * 2 + z) * rows + low
            return terms[part, pl.ds(aligned(start), high - low), :]

        own_term = functools.partial(term, zh)
        pair_term = functools.partial(term, 1 - zh)

        for group, (low_at, high_at) in enumerate(GROUPS):

            def hand_over(low_at=low_at, high_at=high_at, pair_term=pair_term, part=part):
                for at in range(low_at, high_at):
                    share_out[part, at] = pair_term(OFFSETS[at], kept, rows).astype(BF16)

            def span_of(ref, part=part, low_at=low_at, count=high_at - low_at):
                return ref.at[part, pl.ds(low_at, count)]

            moves.declare(
                ("handed", part, group),
                functools.partial(span_of, share_out),
                functools.partial(span_of, share_in),
                functools.partial(span_of, share_in),
                pair,
            )
            plan.send(
                ("handed", part, group),
                "z",
                (high_at - low_at) * share * head * 2,
                [ready],
                hand_over,
                0.15,
            )

        def own_extra(offset, part=part):
            return [(share_in.at[part, OFFSETS.index(offset)], kept, rows)]

        def own_needs(offset, low, high, part=part, ready=ready):
            if high <= kept:
                return [ready]
            at = OFFSETS.index(offset)
            group = [low_at <= at < high_at for low_at, high_at in GROUPS].index(True)
            return [ready, ("handed", part, group)]

        chain(
            ("gpair", part),
            pair_term,
            lambda offset: (),
            pair_out.at[part],
            pair_in.at[part],
            kept,
            lambda *a, ready=ready: [ready],
        )
        chain(
            ("gown", part),
            own_term,
            own_extra,
            own_out.at[part],
            own_in.at[part],
            rows,
            own_needs,
        )

        def settle(pair_term=pair_term, part=part):
            added = [(pair_in.at[part, FAR - 1, way], 0, kept) for way in range(2)]

            def store(start, stop, total):
                z_out[part, start:stop, :] = total.astype(BF16)

            pieces(0, kept, pair_term(0, 0, kept), added, store)

        moves.declare(
            ("settled", part),
            functools.partial(lambda at: z_out.at[at], part),
            functools.partial(lambda at: z_in.at[at], part),
            functools.partial(lambda at: z_in.at[at], part),
            pair,
        )
        plan.send(
            ("settled", part),
            "z",
            kept * head * 2,
            last_hops(("gpair", part)),
            settle,
            0.1,
        )

        def update(own_term=own_term, own_extra=own_extra, part=part):
            added = list(own_extra(0)) + [(z_in.at[part], 0, kept)]
            added += [(own_in.at[part, FAR - 1, way], 0, rows) for way in range(2)]
            lanes = slice(part * head, (part + 1) * head)

            def store(start, stop, total):
                moved = MOMENTUM_DECAY * momentum[start:stop, lanes] + total
                stepped = weights_ref[start:stop, lanes] - LEARNING_RATE * moved
                grad_ref[start:stop, lanes] = total
                stepped_ref[start:stop, lanes] = stepped.astype(BF16)

            pieces(0, rows, own_term(0, 0, rows), added, store)

        plan.compute(
            ("update", part),
            0.2,
            last_hops(("gown", part)) + [("settled", part), ("handed", part, 2), "momentum"],
            update,
        )

    plan.compute("momentum", 0.1, (), momentum_copy.wait)
    plan.run(SCATTER_ORDER)
    moves.drain()


def rope_tables(tokens, places, head):
    half = head // 2
    freqs = ROPE_BASE ** (-(np.arange(half, dtype=np.float64) * 2.0 / head))
    freqs = np.concatenate([freqs, freqs])
    near = np.arange(tokens, dtype=np.float64)[:, None] * freqs
    far = (np.arange(places, dtype=np.float64) * tokens)[:, None] * freqs
    return (
        np.stack([np.cos(near), np.sin(near)]).astype(np.float32),
        np.stack([np.cos(far), np.sin(far)]).astype(np.float32),
    )


def passed_along(value, axis, steps):
    count = lax.axis_size(axis)
    pairs = [(source, (source + steps) % count) for source in range(count)]
    return lax.ppermute(value, axis, pairs)


def on_device(activations, weights, momentum, cotangent, step):
    acts = activations[0]
    params = weights[0]
    moment = momentum[0]
    dout = cotangent[0]
    tokens, width = acts.shape
    rows, columns = params.shape
    head = dout.shape[1]
    share = rows // 9 * 2
    kept = rows - share
    near, far = rope_tables(tokens, lax.axis_size("fsdp"), head)
    near, far = jnp.asarray(near), jnp.asarray(far)
    vmem = pl.BlockSpec(memory_space=pltpu.VMEM)
    anywhere = pl.BlockSpec(memory_space=pl.ANY)
    grad, stepped = pl.pallas_call(
        kernel,
        out_shape=[
            jax.ShapeDtypeStruct((rows, columns), F32),
            jax.ShapeDtypeStruct((rows, columns), BF16),
        ],
        in_specs=[anywhere, vmem, anywhere, vmem, vmem, vmem],
        out_specs=[vmem, vmem],
        scratch_shapes=[
            pltpu.VMEM((tokens, width), BF16),
            pltpu.VMEM((width, tokens), BF16),
            pltpu.VMEM((rows, columns), F32),
            pltpu.VMEM((3, width, head), BF16),
            pltpu.VMEM((RING * tokens, head), BF16),
            pltpu.VMEM((RING * tokens, head), BF16),
            pltpu.VMEM((2 * tokens, head), BF16),
            pltpu.VMEM((2 * tokens, head), BF16),
            pltpu.VMEM((RING, 2 * tokens, tokens), F32),
            pltpu.VMEM((RING, 2 * tokens, tokens), F32),
            pltpu.VMEM((RING, 2 * tokens, tokens), F32),
            pltpu.VMEM((2, RING, tokens), F32),
            pltpu.VMEM((2, RING, RING, tokens), F32),
            pltpu.VMEM((RING, tokens), F32),
            pltpu.VMEM((RING, tokens), F32),
            pltpu.VMEM((RING * tokens, head), F32),
            pltpu.VMEM((FAR, 2, tokens, head), BF16),
            pltpu.VMEM((FAR, 2, tokens, head), BF16),
            pltpu.VMEM((2 * tokens, head), F32),
            pltpu.VMEM((2 * tokens, head), F32),
            pltpu.VMEM((2, tokens, head), BF16),
            pltpu.VMEM((2, tokens, head), BF16),
            pltpu.VMEM((3, tokens, head), BF16),
            pltpu.VMEM((3, FAR, 2, rows, head), BF16),
            pltpu.VMEM((3, FAR, 2, rows, head), BF16),
            pltpu.VMEM((3, FAR, 2, kept, head), BF16),
            pltpu.VMEM((3, FAR, 2, kept, head), BF16),
            pltpu.VMEM((3, RING, share, head), BF16),
            pltpu.VMEM((3, RING, share, head), BF16),
            pltpu.VMEM((3, kept, head), BF16),
            pltpu.VMEM((3, kept, head), BF16),
            pltpu.VMEM((3, width, head), F32),
            pltpu.SemaphoreType.DMA((SEMS,)),
            pltpu.SemaphoreType.DMA((SEMS,)),
            pltpu.SemaphoreType.DMA((2,)),
        ],
        compiler_params=pltpu.CompilerParams(
            collective_id=0, has_side_effects=True, vmem_limit_bytes=56 * 2**20
        ),
        name="attention_step",
    )(acts, params, moment, dout, near, far)
    replicas = lax.axis_size("rep")
    branches = [
        functools.partial(passed_along, axis="rep", steps=2**level % replicas)
        for level in range(PERIOD)
    ]
    partner = lax.switch(step[0] % PERIOD, branches, stepped).astype(F32)
    new_moment = MOMENTUM_DECAY * moment + grad
    new_weights = (params - LEARNING_RATE * new_moment + partner) * 0.5
    return (new_weights[None], new_moment[None])


def solution(mesh):
    spec = P("rep", "fsdp", None)
    return jax.shard_map(
        on_device,
        mesh=mesh,
        in_specs=(spec, spec, spec, spec, P()),
        out_specs=(spec, spec),
        check_vma=False,
    )
```

time: 776 us -> 133 us (0.17)
  the two profiles are of different devices: /device:TPU:16 before, /device:TPU:8 now
where the time goes in v2:
time: 133 us
  Pallas kernels  113 us (85%)
  waiting for transfers between devices  8.69 us (7%)
  starting transfers between devices  7.38 us (6%)
  other arithmetic  2.08 us (2%)
  between operations  1.4 us (1%)
    pallas_call x1, Pallas kernels, on_device(): pl.pallas_call(kernel, out_shape=[jax.ShapeDtypeStruct((rows, columns), F...  113 us
    ppermute x1, waiting for transfers between devices, passed_along(): return lax.ppermute(value, axis, pairs)  8.69 us
    ppermute x1, starting transfers between devices, passed_along(): return lax.ppermute(value, axis, pairs)  7.38 us
  transfers between devices with their start and end apart: 1, of which 1 were waited for; matrix products, arithmetic and copies ran while one was open for 0% of the time, Pallas kernels for 0%

profile of v2, /device:TPU:8, one launch (start us, length us, event | category | flops | bytes accessed | tf_op | source)
XLA Modules:
  0.0 132.9 jit_solution(9963396066643764584)
XLA Ops:
  0.6 0.0 copy-start.1
  0.6 0.0 copy-start
  1.4 113.3 %attention_step.1 = (f32[288,384]{1,0:T(8,128)}, bf16[288,384]{1,0:T(8,128)(2,1)S(1)}) custom-call(bf16[256,4608]{1,0:T(8,128)(2,1)} %bitcast.15, f32[288,384]{1,0:T(8,128)} %bitcast.16, f32[288,384]{1,0:T(8,128)} %bitcast.17, bf16[256,128]{1,0:T(8,128)(2,1)} %bitcast.18, f32[2,256,128]{2,1,0:T(8,128)} %constant.23.clone.near_ref, ...), custom_call_target="tpu_custom_call" | custom-call | tf_op jit(solution)/shard_map/attention_step/pallas_call | solution.py:673
  114.7 16.1 %conditional.4 = (bf16[288,384]{1,0:T(8,128)(2,1)}) conditional(s32[]{:T(128)} %clamp.3, bf16[288,384]{1,0:T(8,128)(2,1)S(1)} %get-tuple-element.20, bf16[288,384]{1,0:T(8,128)(2,1)S(1)} %get-tuple-element.20, bf16[288,384]{1,0:T(8,128)(2,1)S(1)} %get-tuple-element.20, bf16[288,384]{1,0:T(8,128)(2,1)S(1)} %get-tuple-element.20), branch_computations={%region_0.1_spmd, %region_1.2_spmd, %region_2.3_spmd, %region_3.4_... | conditional | bytes 884784
  114.7 7.4 %collective-permute-start.2 = (bf16[288,384]{1,0:T(8,128)(2,1)S(1)}, bf16[288,384]{1,0:T(8,128)(2,1)}, u32[]{:S(2)}, u32[]{:S(2)}) collective-permute-start(bf16[288,384]{1,0:T(8,128)(2,1)S(1)} %param.2), channel_id=1, source_target_pairs={{0,64},{16,80},{32,96},{48,112},{64,128},{80,144},{96,160},{112,17... | collective-permute-start | bytes 663560 | tf_op jit(solution)/shard_map/cond/branch_2_fun/ppermute | solution.py:656
  122.1 8.7 %collective-permute-done.2 = bf16[288,384]{1,0:T(8,128)(2,1)} collective-permute-done((bf16[288,384]{1,0:T(8,128)(2,1)S(1)}, bf16[288,384]{1,0:T(8,128)(2,1)}, u32[]{:S(2)}, u32[]{:S(2)}) %collective-permute-start.2) | collective-permute-done | bytes 221216 | tf_op jit(solution)/shard_map/cond/branch_2_fun/ppermute | solution.py:656
  130.8 0.0 copy-done.1
  130.8 0.0 copy-done
  130.8 2.1 %fusion = (f32[1,288,384]{2,1,0:T(8,128)}, f32[1,288,384]{2,1,0:T(8,128)}) fusion(f32[288,384]{1,0:T(8,128)} %get-tuple-element.19, f32[1,288,384]{2,1,0:T(8,128)S(1)} %copy-done.1, bf16[288,384]{1,0:T(8,128)(2,1)} %get-tuple-element.23, f32[1,288,384]{2,1,0:T(8,128)S(1)} %copy-done), kind=kLoop, calls=%fused_computation.2 | loop fusion | flops 774144 | bytes 2433024 | tf_op jit(solution)/shard_map/broadcast_in_dim | solution.py:731
Async XLA Ops:
  0.6 130.2 %copy-start.1 = (f32[1,288,384]{2,1,0:T(8,128)S(1)}, f32[1,288,384]{2,1,0:T(8,128)}, u32[]{:S(2)}) copy-start(f32[1,288,384]{2,1,0:T(8,128)} %param.13) | copy-start | bytes 1327108
  0.6 130.2 %copy-start = (f32[1,288,384]{2,1,0:T(8,128)S(1)}, f32[1,288,384]{2,1,0:T(8,128)}, u32[]{:S(2)}) copy-start(f32[1,288,384]{2,1,0:T(8,128)} %param.12) | copy-start | bytes 1327108
  114.7 16.1 %collective-permute-start.2 = (bf16[288,384]{1,0:T(8,128)(2,1)S(1)}, bf16[288,384]{1,0:T(8,128)(2,1)}, u32[]{:S(2)}, u32[]{:S(2)}) collective-permute-start(bf16[288,384]{1,0:T(8,128)(2,1)S(1)} %param.2), channel_id=1, source_target_pairs={{0,64},{16,80},{32,96},{48,112},{64,128},{80,144},{96,160},{112,17... | collective-permute-start | bytes 663560 | tf_op jit(solution)/shard_map/cond/branch_2_fun/ppermute | solution.py:656

commit v3 on v2

--- a/solution.py
+++ b/solution.py
@@ -16,6 +16,9 @@
 LEARNING_RATE = 0.5
 RING = 8
 FAR = RING // 2
+GATHER_SHARE = 3
+SCATTER_SHARE = 3
+STRIDES = True
 BF16 = jnp.bfloat16
 F32 = jnp.float32
 MESH = pl.DeviceIdType.MESH
@@ -24,18 +27,18 @@
 GROUPS = ((0, 3), (3, 5), (5, 8))
 
 GATHER_ORDER = (
-    1, 27, 0, 91, 99, 51, 2, 101, 94, 92, 93, 50, 97, 52, 26, 100, 103, 102, 96, 95,
-    75, 76, 98, 25, 3, 29, 19, 9, 4, 17, 28, 18, 10, 67, 69, 59, 54, 42, 34, 20,
-    35, 46, 11, 21, 6, 68, 5, 45, 12, 43, 61, 71, 60, 44, 36, 37, 13, 31, 23, 53,
-    22, 14, 7, 8, 30, 62, 15, 56, 38, 48, 70, 33, 55, 16, 24, 39, 63, 47, 64, 77,
-    73, 58, 32, 49, 78, 40, 104, 85, 41, 72, 86, 74, 65, 57, 66, 79, 80, 105, 106, 83,
-    84, 89, 88, 107, 108, 87, 90, 81, 82,
+    0, 2, 26, 91, 95, 99, 98, 97, 51, 52, 50, 103, 102, 93, 94, 27, 1, 100, 92, 101,
+    25, 96, 76, 75, 4, 19, 28, 42, 54, 9, 18, 3, 10, 17, 29, 59, 67, 21, 30, 35,
+    43, 6, 34, 71, 11, 12, 20, 5, 31, 46, 47, 53, 56, 45, 61, 8, 23, 13, 37, 44,
+    36, 60, 22, 7, 14, 48, 55, 33, 24, 58, 15, 73, 39, 63, 68, 62, 38, 70, 16, 77,
+    78, 49, 57, 74, 41, 32, 72, 65, 64, 40, 104, 85, 86, 69, 79, 66, 105, 80, 106, 83,
+    84, 89, 90, 107, 108, 81, 88, 87, 82,
 )
 SCATTER_ORDER = (
-    3, 2, 77, 1, 0, 7, 6, 8, 11, 12, 23, 16, 15, 13, 9, 33, 5, 4, 34, 35,
-    38, 45, 18, 37, 36, 17, 24, 25, 14, 46, 10, 40, 55, 60, 59, 20, 56, 39, 26, 67,
-    57, 19, 48, 27, 58, 62, 61, 42, 41, 68, 21, 22, 47, 28, 63, 64, 69, 70, 31, 43,
-    44, 49, 50, 65, 66, 71, 72, 53, 29, 30, 51, 52, 75, 73, 74, 32, 54, 76,
+    1, 0, 3, 2, 8, 9, 7, 6, 79, 10, 13, 14, 5, 4, 18, 17, 16, 25, 11, 35,
+    40, 39, 47, 36, 20, 19, 12, 57, 62, 26, 58, 41, 61, 42, 27, 22, 21, 64, 59, 69,
+    28, 43, 44, 37, 63, 48, 49, 24, 15, 66, 23, 70, 71, 60, 46, 50, 65, 45, 38, 68,
+    51, 72, 73, 30, 33, 67, 52, 29, 55, 74, 75, 32, 77, 53, 54, 31, 76, 56, 34, 78,
 )
 
 
@@ -120,8 +123,8 @@
     weights_ref,
     momentum_hbm,
     dout_ref,
-    near_ref,
-    far_ref,
+    near_hbm,
+    far_hbm,
     grad_ref,
     stepped_ref,
     acts,
@@ -146,6 +149,7 @@
     dv_acc,
     dkv_out,
     dkv_in,
+    dscore_buf,
     dproj,
     own_out,
     own_in,
@@ -156,6 +160,8 @@
     z_out,
     z_in,
     terms,
+    near_ref,
+    far_ref,
     send_sem,
     recv_sem,
     local_sem,
@@ -163,7 +169,7 @@
     rows = weights_ref.shape[0]
     tokens, head = dout_ref.shape
     width = acts.shape[1]
-    share = rows // 9 * 2
+    share = rows // 9 * GATHER_SHARE
     kept = rows - share
     qscale = float(width // HEADS) ** (-0.5)
     pscale = float(width) ** (-0.5)
@@ -184,6 +190,10 @@
     acts_copy.start()
     momentum_copy = pltpu.make_async_copy(momentum_hbm, momentum, local_sem.at[1])
     momentum_copy.start()
+    near_copy = pltpu.make_async_copy(near_hbm, near_ref, local_sem.at[2])
+    near_copy.start()
+    far_copy = pltpu.make_async_copy(far_hbm, far_ref, local_sem.at[3])
+    far_copy.start()
 
     barrier = pltpu.get_barrier_semaphore()
     greeted = [column(step) for step in range(1, RING)] + [pair]
@@ -267,14 +277,13 @@
         return buffer.at[pl.ds(aligned(around(step) * tokens + low), high - low), :]
 
     gather(plan, "dout", functools.partial(block_view, dout_all), tokens, ())
-    gather(plan, "query", functools.partial(block_view, query_all), tokens, ["query"], True)
+    gather(plan, "query", functools.partial(block_view, query_all), tokens, ["query"], STRIDES)
 
     half_head = head // 2
-    far_cos = far_ref[0, pl.ds(place, 1), :]
-    far_sin = far_ref[1, pl.ds(place, 1), :]
 
     def turned_by(matrix, direction):
         near_cos, near_sin = near_ref[0], near_ref[1]
+        far_cos, far_sin = far_ref[0, pl.ds(place, 1), :], far_ref[1, pl.ds(place, 1), :]
         cosine = near_cos * far_cos - near_sin * far_sin
         sine = near_sin * far_cos + near_cos * far_sin
         lane = lax.broadcasted_iota(jnp.int32, (tokens, head), 1)
@@ -307,7 +316,12 @@
             at = pl.multiple_of(t * tile, tile)
             acts_t[pl.ds(at, tile), :] = acts[:, pl.ds(at, tile)].T
 
-    plan.compute("acts", 0.1, (), acts_copy.wait)
+    def loaded():
+        acts_copy.wait()
+        near_copy.wait()
+        far_copy.wait()
+
+    plan.compute("acts", 0.1, (), loaded)
     for at in range(turns):
         plan.compute(("turn", at), 0.25, ["acts"], functools.partial(turn, at))
     plan.compute("query", 1.0, arrivals[0] + ["acts"], make_query)
@@ -395,24 +409,20 @@
             span = slice(low, low + sub)
             dv_acc[span, :] += dot_nn((expo_buf[block, span, :] * inv).astype(BF16), dout)
 
-    def swap(kind, acc):
-        dkv_out[kind] = acc[their_rows, :].astype(BF16)
+    for kind in range(2):
         moves.declare(
             ("swap", kind),
-            lambda: dkv_out.at[kind],
-            lambda: dkv_in.at[kind],
-            lambda: dkv_in.at[kind],
+            functools.partial(lambda at: dkv_out.at[at], kind),
+            functools.partial(lambda at: dkv_in.at[at], kind),
+            functools.partial(lambda at: dkv_in.at[at], kind),
             pair,
         )
-        moves.start(("swap", kind))
-
-    swap(1, dv_acc)
+    dkv_out[1] = dv_acc[their_rows, :].astype(BF16)
+    moves.start(("swap", 1))
     delta_buf[...] = summed(1) * inverse
 
     @pl.loop(y, RING)
     def _(block):
-        at = pl.ds(aligned(block * tokens), tokens)
-        query = query_all[at, :]
         inv = inv_buf[pl.ds(block, 1), :] * qscale
         delta = delta_buf[pl.ds(block, 1), :]
         dquery = jnp.zeros((tokens, head), F32)
@@ -420,11 +430,19 @@
             span = slice(low, low + sub)
             dscore = slope_buf[block, span, :] * (dprob_buf[block, span, :] - delta) * inv
             dscore = dscore.astype(BF16)
-            dk_acc[span, :] += dot_nn(dscore, query)
+            dscore_buf[block, span, :] = dscore
             dquery += dot_tn(dscore, keys[span, :])
-        dq_buf[at, :] = dquery
-
-    swap(0, dk_acc)
+        dq_buf[pl.ds(aligned(block * tokens), tokens), :] = dquery
+
+    def make_dk():
+        @pl.loop(y, RING)
+        def _(block):
+            query = query_all[pl.ds(aligned(block * tokens), tokens), :]
+            for low in range(0, 2 * tokens, sub):
+                span = slice(low, low + sub)
+                dk_acc[span, :] += dot_nn(dscore_buf[block, span, :], query)
+
+        dkv_out[0] = dk_acc[their_rows, :].astype(BF16)
 
     plan = Plan(moves)
 
@@ -511,6 +529,8 @@
             total += dq_in[2, way].astype(F32) + dq_in[3, way].astype(F32)
         dproj[0] = turned_by(total, -1.0).astype(BF16)
 
+    plan.compute("dk", 1.2, (), make_dk)
+    plan.send(("swap", 0), "z", tokens * head * 2, ["dk"])
     plan.compute(("dproj", 2), 0.2, [("swap", 1)], finish_dv)
     plan.compute(("dproj", 1), 0.3, [("swap", 0)], finish_dk)
     plan.compute(("dproj", 0), 0.4, [("dquery", step, way) for step in (2, 3) for way in range(2)], finish_dq)
@@ -664,7 +684,7 @@
     tokens, width = acts.shape
     rows, columns = params.shape
     head = dout.shape[1]
-    share = rows // 9 * 2
+    share = rows // 9 * SCATTER_SHARE
     kept = rows - share
     near, far = rope_tables(tokens, lax.axis_size("fsdp"), head)
     near, far = jnp.asarray(near), jnp.asarray(far)
@@ -676,7 +696,7 @@
             jax.ShapeDtypeStruct((rows, columns), F32),
             jax.ShapeDtypeStruct((rows, columns), BF16),
         ],
-        in_specs=[anywhere, vmem, anywhere, vmem, vmem, vmem],
+        in_specs=[anywhere, vmem, anywhere, vmem, anywhere, anywhere],
         out_specs=[vmem, vmem],
         scratch_shapes=[
             pltpu.VMEM((tokens, width), BF16),
@@ -701,6 +721,7 @@
             pltpu.VMEM((2 * tokens, head), F32),
             pltpu.VMEM((2, tokens, head), BF16),
             pltpu.VMEM((2, tokens, head), BF16),
+            pltpu.VMEM((RING, 2 * tokens, tokens), BF16),
             pltpu.VMEM((3, tokens, head), BF16),
             pltpu.VMEM((3, FAR, 2, rows, head), BF16),
             pltpu.VMEM((3, FAR, 2, rows, head), BF16),
@@ -711,9 +732,11 @@
             pltpu.VMEM((3, kept, head), BF16),
             pltpu.VMEM((3, kept, head), BF16),
             pltpu.VMEM((3, width, head), F32),
+            pltpu.VMEM(near.shape, F32),
+            pltpu.VMEM(far.shape, F32),
             pltpu.SemaphoreType.DMA((SEMS,)),
             pltpu.SemaphoreType.DMA((SEMS,)),
-            pltpu.SemaphoreType.DMA((2,)),
+            pltpu.SemaphoreType.DMA((4,)),
         ],
         compiler_params=pltpu.CompilerParams(
             collective_id=0, has_side_effects=True, vmem_limit_bytes=56 * 2**20

time: 133 us -> 127 us (0.955)
  Pallas kernels: 113 us -> 109 us
  starting transfers between devices: 7.38 us -> 3.87 us
    pallas_call x1, Pallas kernels: 113 us -> 109 us  [on_device(): pl.pallas_call(kernel, out_shape=[jax.ShapeDtypeStruct((rows, columns), F...]
    ppermute x1, starting transfers between devices: 7.38 us -> 3.87 us  [passed_along(): return lax.ppermute(value, axis, pairs)]
where the time goes in v3:
time: 127 us; the launch traced here: 126 us
  Pallas kernels  109 us (86%)
  waiting for transfers between devices  8.93 us (7%)
  starting transfers between devices  3.87 us (3%)
  other arithmetic  2.08 us (2%)
  between operations  1.4 us (1%)
    pallas_call x1, Pallas kernels, on_device(): pl.pallas_call(kernel, out_shape=[jax.ShapeDtypeStruct((rows, columns), F...  109 us
    ppermute x1, waiting for transfers between devices, passed_along(): return lax.ppermute(value, axis, pairs)  8.93 us
    ppermute x1, starting transfers between devices, passed_along(): return lax.ppermute(value, axis, pairs)  3.87 us
  transfers between devices with their start and end apart: 1, of which 1 were waited for; matrix products, arithmetic and copies ran while one was open for 0% of the time, Pallas kernels for 0%

profile of v3, /device:TPU:8, one launch (start us, length us, event | category | flops | bytes accessed | tf_op | source)
XLA Modules:
  0.0 125.8 jit_solution(7909114645690756106)
XLA Ops:
  0.6 0.0 copy-start.1
  0.6 0.0 copy-start
  1.4 109.5 %attention_step.1 = (f32[288,384]{1,0:T(8,128)}, bf16[288,384]{1,0:T(8,128)(2,1)S(1)}) custom-call(bf16[256,4608]{1,0:T(8,128)(2,1)} %bitcast.15, f32[288,384]{1,0:T(8,128)} %bitcast.16, f32[288,384]{1,0:T(8,128)} %bitcast.17, bf16[256,128]{1,0:T(8,128)(2,1)} %bitcast.18, f32[2,256,128]{2,1,0:T(8,128)} %constant.23.clone.near_hbm, ...), custom_call_target="tpu_custom_call" | custom-call | tf_op jit(solution)/shard_map/attention_step/pallas_call | solution.py:693
  110.9 12.8 %conditional.4 = (bf16[288,384]{1,0:T(8,128)(2,1)}) conditional(s32[]{:T(128)} %clamp.3, bf16[288,384]{1,0:T(8,128)(2,1)S(1)} %get-tuple-element.20, bf16[288,384]{1,0:T(8,128)(2,1)S(1)} %get-tuple-element.20, bf16[288,384]{1,0:T(8,128)(2,1)S(1)} %get-tuple-element.20, bf16[288,384]{1,0:T(8,128)(2,1)S(1)} %get-tuple-element.20), branch_computations={%region_0.1_spmd, %region_1.2_spmd, %region_2.3_spmd, %region_3.4_... | conditional | bytes 884784
  110.9 3.9 %collective-permute-start.1 = (bf16[288,384]{1,0:T(8,128)(2,1)S(1)}, bf16[288,384]{1,0:T(8,128)(2,1)}, u32[]{:S(2)}, u32[]{:S(2)}) collective-permute-start(bf16[288,384]{1,0:T(8,128)(2,1)S(1)} %param.1), channel_id=1, source_target_pairs={{0,32},{16,48},{32,64},{48,80},{64,96},{80,112},{96,128},{112,144}... | collective-permute-start | bytes 663560 | tf_op jit(solution)/shard_map/cond/branch_1_fun/ppermute | solution.py:676
  114.8 8.9 %collective-permute-done.1 = bf16[288,384]{1,0:T(8,128)(2,1)} collective-permute-done((bf16[288,384]{1,0:T(8,128)(2,1)S(1)}, bf16[288,384]{1,0:T(8,128)(2,1)}, u32[]{:S(2)}, u32[]{:S(2)}) %collective-permute-start.1) | collective-permute-done | bytes 221216 | tf_op jit(solution)/shard_map/cond/branch_1_fun/ppermute | solution.py:676
  123.7 0.0 copy-done.1
  123.7 0.0 copy-done
  123.7 2.1 %fusion = (f32[1,288,384]{2,1,0:T(8,128)}, f32[1,288,384]{2,1,0:T(8,128)}) fusion(f32[288,384]{1,0:T(8,128)} %get-tuple-element.19, f32[1,288,384]{2,1,0:T(8,128)S(1)} %copy-done.1, bf16[288,384]{1,0:T(8,128)(2,1)} %get-tuple-element.23, f32[1,288,384]{2,1,0:T(8,128)S(1)} %copy-done), kind=kLoop, calls=%fused_computation.2 | loop fusion | flops 774144 | bytes 2433024 | tf_op jit(solution)/shard_map/broadcast_in_dim | solution.py:754
Async XLA Ops:
  0.6 123.1 %copy-start.1 = (f32[1,288,384]{2,1,0:T(8,128)S(1)}, f32[1,288,384]{2,1,0:T(8,128)}, u32[]{:S(2)}) copy-start(f32[1,288,384]{2,1,0:T(8,128)} %param.13) | copy-start | bytes 1327108
  0.6 123.1 %copy-start = (f32[1,288,384]{2,1,0:T(8,128)S(1)}, f32[1,288,384]{2,1,0:T(8,128)}, u32[]{:S(2)}) copy-start(f32[1,288,384]{2,1,0:T(8,128)} %param.12) | copy-start | bytes 1327108
  110.9 12.8 %collective-permute-start.1 = (bf16[288,384]{1,0:T(8,128)(2,1)S(1)}, bf16[288,384]{1,0:T(8,128)(2,1)}, u32[]{:S(2)}, u32[]{:S(2)}) collective-permute-start(bf16[288,384]{1,0:T(8,128)(2,1)S(1)} %param.1), channel_id=1, source_target_pairs={{0,32},{16,48},{32,64},{48,80},{64,96},{80,112},{96,128},{112,144}... | collective-permute-start | bytes 663560 | tf_op jit(solution)/shard_map/cond/branch_1_fun/ppermute | solution.py:676

commit v4 on v3

--- a/solution.py
+++ b/solution.py
@@ -125,7 +125,8 @@
     dout_ref,
     near_hbm,
     far_hbm,
-    grad_ref,
+    new_momentum_ref,
+    kept_ref,
     stepped_ref,
     acts,
     acts_t,
@@ -361,7 +362,7 @@
         sums_own[0, pl.ds(block, 1), :] = total
 
     def exchange(kind):
-        for step in range(1, RING):
+        for step in OFFSETS[:-1]:
             name = ("sums", kind, step)
             moves.declare(
                 name,
@@ -641,7 +642,8 @@
             def store(start, stop, total):
                 moved = MOMENTUM_DECAY * momentum[start:stop, lanes] + total
                 stepped = weights_ref[start:stop, lanes] - LEARNING_RATE * moved
-                grad_ref[start:stop, lanes] = total
+                new_momentum_ref[start:stop, lanes] = moved
+                kept_ref[start:stop, lanes] = stepped
                 stepped_ref[start:stop, lanes] = stepped.astype(BF16)
 
             pieces(0, rows, own_term(0, 0, rows), added, store)
@@ -690,14 +692,15 @@
     near, far = jnp.asarray(near), jnp.asarray(far)
     vmem = pl.BlockSpec(memory_space=pltpu.VMEM)
     anywhere = pl.BlockSpec(memory_space=pl.ANY)
-    grad, stepped = pl.pallas_call(
+    new_moment, own_stepped, stepped = pl.pallas_call(
         kernel,
         out_shape=[
+            jax.ShapeDtypeStruct((rows, columns), F32),
             jax.ShapeDtypeStruct((rows, columns), F32),
             jax.ShapeDtypeStruct((rows, columns), BF16),
         ],
         in_specs=[anywhere, vmem, anywhere, vmem, anywhere, anywhere],
-        out_specs=[vmem, vmem],
+        out_specs=[vmem, vmem, vmem],
         scratch_shapes=[
             pltpu.VMEM((tokens, width), BF16),
             pltpu.VMEM((width, tokens), BF16),
@@ -749,8 +752,7 @@
         for level in range(PERIOD)
     ]
     partner = lax.switch(step[0] % PERIOD, branches, stepped).astype(F32)
-    new_moment = MOMENTUM_DECAY * moment + grad
-    new_weights = (params - LEARNING_RATE * new_moment + partner) * 0.5
+    new_weights = (own_stepped + partner) * 0.5
     return (new_weights[None], new_moment[None])
 
 

time: 127 us -> 126 us (level)
  the two profiles are of different devices: /device:TPU:8 before, /device:TPU:24 now
where the time goes in v4:
time: 126 us; the launch traced here: 125 us
  Pallas kernels  111 us (88%)
  waiting for transfers between devices  5.73 us (5%)
  starting transfers between devices  3.41 us (3%)
  other arithmetic  1.88 us (1%)
  local copies, waits for them, and re-layouts  1.8 us (1%)
  between operations  1.3 us (1%)
    pallas_call x1, Pallas kernels, on_device(): pl.pallas_call(kernel, out_shape=[jax.ShapeDtypeStruct((rows, columns), F...  111 us
    ppermute x1, waiting for transfers between devices, passed_along(): return lax.ppermute(value, axis, pairs)  5.73 us
    ppermute x1, starting transfers between devices, passed_along(): return lax.ppermute(value, axis, pairs)  3.41 us
  transfers between devices with their start and end apart: 1, of which 1 were waited for; matrix products, arithmetic and copies ran while one was open for 0% of the time, Pallas kernels for 0%

profile of v4, /device:TPU:24, one launch (start us, length us, event | category | flops | bytes accessed | tf_op | source)
XLA Modules:
  0.0 124.7 jit_solution(11577388372776082288)
XLA Ops:
  1.3 110.5 %attention_step.1 = (f32[288,384]{1,0:T(8,128)}, f32[288,384]{1,0:T(8,128)}, bf16[288,384]{1,0:T(8,128)(2,1)S(1)}) custom-call(bf16[256,4608]{1,0:T(8,128)(2,1)} %bitcast.11, f32[288,384]{1,0:T(8,128)} %bitcast.12, f32[288,384]{1,0:T(8,128)} %bitcast.13, bf16[256,128]{1,0:T(8,128)(2,1)} %bitcast.15, f32[2,256,128]{2,1,0:T(8,128)} %constant.21.clone.near_hbm, ...), custom_call_target="tpu_custom_call" | custom-call | tf_op jit(solution)/shard_map/attention_step/pallas_call | solution.py:695
  111.8 9.2 %conditional.4 = (bf16[288,384]{1,0:T(8,128)(2,1)}) conditional(s32[]{:T(128)} %clamp.3, bf16[288,384]{1,0:T(8,128)(2,1)S(1)} %get-tuple-element.21, bf16[288,384]{1,0:T(8,128)(2,1)S(1)} %get-tuple-element.21, bf16[288,384]{1,0:T(8,128)(2,1)S(1)} %get-tuple-element.21, bf16[288,384]{1,0:T(8,128)(2,1)S(1)} %get-tuple-element.21), branch_computations={%region_0.1_spmd, %region_1.2_spmd, %region_2.3_spmd, %region_3.4_... | conditional | bytes 884784
  111.9 3.4 %collective-permute-start.3 = (bf16[288,384]{1,0:T(8,128)(2,1)S(1)}, bf16[288,384]{1,0:T(8,128)(2,1)}, u32[]{:S(2)}, u32[]{:S(2)}) collective-permute-start(bf16[288,384]{1,0:T(8,128)(2,1)S(1)} %param.3), channel_id=1, source_target_pairs={{0,128},{16,144},{32,160},{48,176},{64,192},{80,208},{96,224},{112... | collective-permute-start | bytes 663560 | tf_op jit(solution)/shard_map/cond/branch_3_fun/ppermute | solution.py:678
  115.3 5.7 %collective-permute-done.3 = bf16[288,384]{1,0:T(8,128)(2,1)} collective-permute-done((bf16[288,384]{1,0:T(8,128)(2,1)S(1)}, bf16[288,384]{1,0:T(8,128)(2,1)}, u32[]{:S(2)}, u32[]{:S(2)}) %collective-permute-start.3) | collective-permute-done | bytes 221216 | tf_op jit(solution)/shard_map/cond/branch_3_fun/ppermute | solution.py:678
  121.0 1.9 %multiply_bitcast_fusion = f32[1,288,384]{2,1,0:T(8,128)} fusion(f32[288,384]{1,0:T(8,128)} %get-tuple-element.20, bf16[288,384]{1,0:T(8,128)(2,1)} %get-tuple-element.27), kind=kLoop, calls=%fused_computation | loop fusion | flops 331776 | bytes 1105920 | tf_op jit(solution)/shard_map/broadcast_in_dim | solution.py:756
  122.9 1.8 %copy.15 = f32[1,288,384]{2,1,0:T(8,128)} copy(f32[1,288,384]{2,1,0:T(8,128)} %bitcast.14) | data formatting | bytes 884736
Async XLA Ops:
  111.9 9.1 %collective-permute-start.3 = (bf16[288,384]{1,0:T(8,128)(2,1)S(1)}, bf16[288,384]{1,0:T(8,128)(2,1)}, u32[]{:S(2)}, u32[]{:S(2)}) collective-permute-start(bf16[288,384]{1,0:T(8,128)(2,1)S(1)} %param.3), channel_id=1, source_target_pairs={{0,128},{16,144},{32,160},{48,176},{64,192},{80,208},{96,224},{112... | collective-permute-start | bytes 663560 | tf_op jit(solution)/shard_map/cond/branch_3_fun/ppermute | solution.py:678
